TPU v7x, 256 devices: a whole 4x4x8 slice. The times are simulated.
256 devices in a mesh: aux: 8 (over x, y_hi), occ: 16 (over z, core), pair: 2 (over y_lo).
Axes of the slice: x: 4, y: 4 (y_hi: 2, y_lo: 2; y = y_hi * 2 + y_lo), z: 8, core: 2. Of those that a mesh axis runs over, the one named last changes fastest.
Arguments:
- first_factors: bfloat16 [4096, 2, 4096], P(('aux', 'occ')), may hold values from -0.75 to 0.75
- second_factors: bfloat16 [4096, 32, 4096], P(('aux', 'occ', 'pair')), may hold values from -0.75 to 0.75
- first_energy: float32 [2], replicated, may hold values from -1.2 to -0.3
- second_energy: float32 [32], P(('occ', 'pair')), may hold values from -1.2 to -0.3
- virtual_energy: float32 [4096], replicated, may hold values from 0.2 to 4
- kept_blocks: int32 [2, 32, 64, 2], P(None, ('occ', 'pair')), may hold values from 0 to 63, all different within a row
Outputs:
- first_density: bfloat16 [4096, 2, 4096], P('aux', 'pair', 'occ')
- second_density: bfloat16 [4096, 32, 4096], P('aux', ('occ', 'pair'))
Inputs may be any that keep to these rules, and one draw needn't show every extreme that they name: Each row kept_blocks[i, j, A, :] names 2 different blocks.
All inputs are finite; a program needn't handle non-finite values.
Results may differ from a plain program's by a relative error of at most 0.0048.
Values may be sent and summed in bfloat16 or wider, within the bound.
A program may use at most 128 MiB of HBM per device.

v0:
```python
import jax
import jax.numpy as jnp
from jax import lax
from jax.sharding import PartitionSpec as P

BLK = 64


def from_behind(x, axis, by):
    peers = lax.axis_size(axis)
    return lax.ppermute(x, axis, [(i, (i + by) % peers) for i in range(peers)])


def block_terms(
    slab_rows,
    anchor,
    kept_local,
    second_blocks,
    first_energy,
    energy_second,
    virtual_energy,
    second_total,
):
    aux_rows, count_first, slab_width = slab_rows.shape
    per_slab = slab_width // BLK
    kept_count = kept_local.shape[2]
    picked = lax.dynamic_slice_in_dim(kept_local, anchor * per_slab, per_slab, 1)
    flat_picks = picked.reshape(-1)
    block_count = flat_picks.shape[0]
    left_rows = jnp.broadcast_to(
        slab_rows.reshape(aux_rows, count_first, per_slab, 1, BLK),
        (aux_rows, count_first, per_slab, kept_count, BLK),
    ).reshape(aux_rows, block_count, BLK)
    right_rows = jnp.take(second_blocks, flat_picks, axis=1)
    partial_intersection = jnp.einsum(
        "pna,pnb->nab", left_rows, right_rows, preferred_element_type=jnp.float32
    )
    intersection = lax.psum(partial_intersection, "aux")
    energy_left = lax.dynamic_slice_in_dim(virtual_energy, anchor * slab_width, slab_width).reshape(
        1, per_slab, 1, BLK
    )
    energy_left = jnp.broadcast_to(energy_left, (count_first, per_slab, kept_count, BLK)).reshape(
        block_count, BLK
    )
    energy_right = jnp.take(virtual_energy.reshape(-1, BLK), flat_picks, axis=0)
    energy_first = jnp.broadcast_to(
        first_energy.reshape(count_first, 1, 1), (count_first, per_slab, kept_count)
    ).reshape(block_count)
    divisor = (
        energy_left[:, :, None]
        + energy_right[:, None, :]
        - energy_first[:, None, None]
        - energy_second
    )
    amplitude = (intersection / divisor).astype(jnp.bfloat16)
    toward_first = jnp.einsum(
        "nab,pnb->pna", amplitude, right_rows, preferred_element_type=jnp.float32
    )
    toward_first = (
        toward_first.reshape(aux_rows, count_first, per_slab, kept_count, BLK)
        .sum(axis=3)
        .reshape(aux_rows, count_first, slab_width)
    )
    toward_second = jnp.einsum(
        "nab,pna->pnb", amplitude, left_rows, preferred_element_type=jnp.float32
    )
    second_total = second_total.at[:, flat_picks, :].add(toward_second)
    return (toward_first, second_total)


def pass_density(carried):
    return from_behind(carried, "occ", 1)


def shards(first_factors, second_factors, first_energy, second_energy, virtual_energy, kept_blocks):
    first_slab = lax.all_to_all(first_factors, "occ", split_axis=2, concat_axis=0, tiled=True)
    second_rows = lax.all_to_all(
        second_factors, ("occ", "pair"), split_axis=1, concat_axis=0, tiled=True
    )
    aux_rows, count_first, slab_width = first_slab.shape
    width = second_rows.shape[2]
    second_blocks = second_rows.reshape(aux_rows, width // BLK, BLK)
    kept_local = kept_blocks[:, 0]
    energy_second = second_energy[0]
    group_size = lax.axis_size("occ")
    here_index = lax.axis_index("occ")
    second_start = jnp.zeros((aux_rows, width // BLK, BLK), jnp.float32)

    def compute(slab_rows, anchor, second_total):
        return block_terms(
            slab_rows,
            anchor,
            kept_local,
            second_blocks,
            first_energy,
            energy_second,
            virtual_energy,
            second_total,
        )

    def advance(position, carried_state):
        slab_rows, carried, second_total = carried_state
        anchor = (here_index - position) % group_size
        toward_first, second_total = compute(slab_rows, anchor, second_total)
        carried = pass_density(carried + toward_first)
        slab_rows = from_behind(slab_rows, "occ", 1)
        return (slab_rows, carried, second_total)

    start_state = (first_slab, jnp.zeros(first_slab.shape, jnp.float32), second_start)
    slab_rows, carried, second_total = lax.fori_loop(0, group_size - 1, advance, start_state)
    anchor = (here_index + 1) % group_size
    toward_first, second_total = compute(slab_rows, anchor, second_total)
    first_sum = pass_density(carried + toward_first)
    first_density = lax.psum_scatter(first_sum, "pair", scatter_dimension=1, tiled=True).astype(
        jnp.bfloat16
    )
    second_density = second_total.reshape(aux_rows, 1, width).astype(jnp.bfloat16)
    return (first_density, second_density)


def solution(mesh):
    placed = (
        P(("aux", "occ"), None, None),
        P(("aux", "occ", "pair"), None, None),
        P(),
        P(("occ", "pair")),
        P(),
        P(None, ("occ", "pair"), None, None),
    )
    return jax.shard_map(
        shards,
        mesh=mesh,
        in_specs=placed,
        out_specs=(P("aux", "pair", "occ"), P("aux", ("occ", "pair"), None)),
        check_vma=False,
    )
```

profile of v0, /device:TPU:29, one launch (start us, length us, event | category | flops | bytes accessed | tf_op | source)
XLA Modules:
  0.0 2150.4 jit_solution(14557512431779156673)
XLA Ops:
  50.3 89.9 %all-to-all-done.1 = bf16[16,32,4096]{2,0,1:T(8,128)(2,1)} async-done(((bf16[16,32,4096]{2,0,1:T(8,128)(2,1)}), bf16[16,32,4096]{2,0,1:T(8,128)(2,1)}, u32[]{:S(2)}, u32[]{:S(2)}) %all-to-all-start.1) | async-done | bytes 4194336 | tf_op jit(solution)/shard_map/all_to_all | solution.py:77
  140.2 12.6 reshape.198
  171.7 1829.5 %while.19 = (s32[]{:T(128)}, bf16[512,2,256]{0,2,1:T(8,128)(2,1)}, f32[512,2,256]{0,2,1:T(8,128)}, f32[512,64,64]{0,2,1:T(8,128)}, s32[]{:T(128)}, /*index=5*/s3...) while((s32[]{:T(128)}, bf16[512,2,256]{0,2,1:T(8,128)(2,1)}, ...), condition=%wide.region_4.7_spmd, body=%wide.region_0.6_spmd.sunk | while | flops 204146896 | bytes 30751560 | solution.py:110
  180.0 79.9 %all-reduce.5.cloned.1.call-done = f32[16,64,64]{1,2,0:T(8,128)} async-done(((f32[16,64,64]{1,2,0:T(8,128)}), f32[16,64,64]{1,2,0:T(8,128)}) %all-reduce.5.cloned.1.call-update) | async-done | bytes 262160 | tf_op jit(solution)/shard_map/while/body/eval_jaxpr/psum | solution.py:38
  278.2 10.9 collective-permute-done
  297.4 84.9 %all-reduce.5.cloned.1.call-done = f32[16,64,64]{1,2,0:T(8,128)} async-done(((f32[16,64,64]{1,2,0:T(8,128)}), f32[16,64,64]{1,2,0:T(8,128)}) %all-reduce.5.cloned.1.call-update) | async-done | bytes 262160 | tf_op jit(solution)/shard_map/while/body/eval_jaxpr/psum | solution.py:38
  419.7 84.9 %all-reduce.5.cloned.1.call-done = f32[16,64,64]{1,2,0:T(8,128)} async-done(((f32[16,64,64]{1,2,0:T(8,128)}), f32[16,64,64]{1,2,0:T(8,128)}) %all-reduce.5.cloned.1.call-update) | async-done | bytes 262160 | tf_op jit(solution)/shard_map/while/body/eval_jaxpr/psum | solution.py:38
  542.0 84.9 %all-reduce.5.cloned.1.call-done = f32[16,64,64]{1,2,0:T(8,128)} async-done(((f32[16,64,64]{1,2,0:T(8,128)}), f32[16,64,64]{1,2,0:T(8,128)}) %all-reduce.5.cloned.1.call-update) | async-done | bytes 262160 | tf_op jit(solution)/shard_map/while/body/eval_jaxpr/psum | solution.py:38
  664.2 85.0 %all-reduce.5.cloned.1.call-done = f32[16,64,64]{1,2,0:T(8,128)} async-done(((f32[16,64,64]{1,2,0:T(8,128)}), f32[16,64,64]{1,2,0:T(8,128)}) %all-reduce.5.cloned.1.call-update) | async-done | bytes 262160 | tf_op jit(solution)/shard_map/while/body/eval_jaxpr/psum | solution.py:38
  767.4 10.9 collective-permute-done
  786.6 84.9 %all-reduce.5.cloned.1.call-done = f32[16,64,64]{1,2,0:T(8,128)} async-done(((f32[16,64,64]{1,2,0:T(8,128)}), f32[16,64,64]{1,2,0:T(8,128)}) %all-reduce.5.cloned.1.call-update) | async-done | bytes 262160 | tf_op jit(solution)/shard_map/while/body/eval_jaxpr/psum | solution.py:38
  908.8 84.9 %all-reduce.5.cloned.1.call-done = f32[16,64,64]{1,2,0:T(8,128)} async-done(((f32[16,64,64]{1,2,0:T(8,128)}), f32[16,64,64]{1,2,0:T(8,128)}) %all-reduce.5.cloned.1.call-update) | async-done | bytes 262160 | tf_op jit(solution)/shard_map/while/body/eval_jaxpr/psum | solution.py:38
  1011.9 10.9 collective-permute-done
  1031.1 85.0 %all-reduce.5.cloned.1.call-done = f32[16,64,64]{1,2,0:T(8,128)} async-done(((f32[16,64,64]{1,2,0:T(8,128)}), f32[16,64,64]{1,2,0:T(8,128)}) %all-reduce.5.cloned.1.call-update) | async-done | bytes 262160 | tf_op jit(solution)/shard_map/while/body/eval_jaxpr/psum | solution.py:38
  1153.5 84.9 %all-reduce.5.cloned.1.call-done = f32[16,64,64]{1,2,0:T(8,128)} async-done(((f32[16,64,64]{1,2,0:T(8,128)}), f32[16,64,64]{1,2,0:T(8,128)}) %all-reduce.5.cloned.1.call-update) | async-done | bytes 262160 | tf_op jit(solution)/shard_map/while/body/eval_jaxpr/psum | solution.py:38
  1275.7 84.9 %all-reduce.5.cloned.1.call-done = f32[16,64,64]{1,2,0:T(8,128)} async-done(((f32[16,64,64]{1,2,0:T(8,128)}), f32[16,64,64]{1,2,0:T(8,128)}) %all-reduce.5.cloned.1.call-update) | async-done | bytes 262160 | tf_op jit(solution)/shard_map/while/body/eval_jaxpr/psum | solution.py:38
  1398.0 85.0 %all-reduce.5.cloned.1.call-done = f32[16,64,64]{1,2,0:T(8,128)} async-done(((f32[16,64,64]{1,2,0:T(8,128)}), f32[16,64,64]{1,2,0:T(8,128)}) %all-reduce.5.cloned.1.call-update) | async-done | bytes 262160 | tf_op jit(solution)/shard_map/while/body/eval_jaxpr/psum | solution.py:38
  1520.3 84.9 %all-reduce.5.cloned.1.call-done = f32[16,64,64]{1,2,0:T(8,128)} async-done(((f32[16,64,64]{1,2,0:T(8,128)}), f32[16,64,64]{1,2,0:T(8,128)}) %all-reduce.5.cloned.1.call-update) | async-done | bytes 262160 | tf_op jit(solution)/shard_map/while/body/eval_jaxpr/psum | solution.py:38
  1642.6 84.9 %all-reduce.5.cloned.1.call-done = f32[16,64,64]{1,2,0:T(8,128)} async-done(((f32[16,64,64]{1,2,0:T(8,128)}), f32[16,64,64]{1,2,0:T(8,128)}) %all-reduce.5.cloned.1.call-update) | async-done | bytes 262160 | tf_op jit(solution)/shard_map/while/body/eval_jaxpr/psum | solution.py:38
  1764.9 85.0 %all-reduce.5.cloned.1.call-done = f32[16,64,64]{1,2,0:T(8,128)} async-done(((f32[16,64,64]{1,2,0:T(8,128)}), f32[16,64,64]{1,2,0:T(8,128)}) %all-reduce.5.cloned.1.call-update) | async-done | bytes 262160 | tf_op jit(solution)/shard_map/while/body/eval_jaxpr/psum | solution.py:38
  1868.1 10.9 collective-permute-done
  1887.2 84.9 %all-reduce.5.cloned.1.call-done = f32[16,64,64]{1,2,0:T(8,128)} async-done(((f32[16,64,64]{1,2,0:T(8,128)}), f32[16,64,64]{1,2,0:T(8,128)}) %all-reduce.5.cloned.1.call-update) | async-done | bytes 262160 | tf_op jit(solution)/shard_map/while/body/eval_jaxpr/psum | solution.py:38
  2006.8 84.3 %all-reduce.3.cloned.1.call-done = f32[16,64,64]{2,1,0:T(8,128)} async-done(((f32[16,64,64]{2,1,0:T(8,128)}), f32[16,64,64]{2,1,0:T(8,128)}) %all-reduce.3.cloned.1.call-update) | async-done | bytes 262160 | tf_op jit(solution)/shard_map/psum | solution.py:38
  2100.5 11.7 collective-permute-done.2
  (487 shorter events, 622.6 us)
Async XLA Ops:
  15.3 26.5 %all-to-all-start = ((bf16[16,2,8192]{2,1,0:T(2,128)(2,1)}), bf16[16,2,8192]{2,1,0:T(2,128)(2,1)S(1)}, u32[]{:S(2)}, u32[]{:S(2)}) async-start(bf16[16,2,8192]{2,1,0:T(2,128)(2,1)} %reshape.265), calls=%async_computation | async-start | bytes 1048576 | tf_op jit(solution)/shard_map/all_to_all | solution.py:76
  41.8 98.4 %all-to-all-start.1 = ((bf16[16,32,4096]{2,0,1:T(8,128)(2,1)}), bf16[16,32,4096]{2,0,1:T(8,128)(2,1)}, u32[]{:S(2)}, u32[]{:S(2)}) async-start(bf16[16,32,4096]{2,0,1:T(8,128)(2,1)} %copy.64), calls=%async_computation.1 | async-start | bytes 8388608 | tf_op jit(solution)/shard_map/all_to_all | solution.py:77
  171.7 88.3 %all-reduce.5.cloned.1.call-start = ((), (), s32[]{:S(2)}) async-start(), calls=%async_computation.5 | async-start | bytes 1048576 | tf_op jit(solution)/shard_map/while/body/eval_jaxpr/psum | solution.py:38
  289.1 93.2 %all-reduce.5.cloned.1.call-start = ((), (), s32[]{:S(2)}) async-start(), calls=%async_computation.5 | async-start | bytes 1048576 | tf_op jit(solution)/shard_map/while/body/eval_jaxpr/psum | solution.py:38
  387.3 24.1 %collective-permute-start.1 = (f32[512,2,256]{0,2,1:T(8,128)}, f32[512,2,256]{0,2,1:T(8,128)}, u32[]{:S(2)}, u32[]{:S(2)}) collective-permute-start(f32[512,2,256]{0,2,1:T(8,128)} %bitcast_add_fusion.3), channel_id=1, source_target_pairs={{0,2},{2,4},{4,6},{6,8},{8,10},{10,12},{12,14},{14,16},{16,18},{18... | collective-permute-start | bytes 3145736 | tf_op jit(solution)/shard_map/while/body/eval_jaxpr/ppermute | solution.py:11
  411.4 93.2 %all-reduce.5.cloned.1.call-start = ((), (), s32[]{:S(2)}) async-start(), calls=%async_computation.5 | async-start | bytes 1048576 | tf_op jit(solution)/shard_map/while/body/eval_jaxpr/psum | solution.py:38
  533.7 93.2 %all-reduce.5.cloned.1.call-start = ((), (), s32[]{:S(2)}) async-start(), calls=%async_computation.5 | async-start | bytes 1048576 | tf_op jit(solution)/shard_map/while/body/eval_jaxpr/psum | solution.py:38
  655.9 93.2 %all-reduce.5.cloned.1.call-start = ((), (), s32[]{:S(2)}) async-start(), calls=%async_computation.5 | async-start | bytes 1048576 | tf_op jit(solution)/shard_map/while/body/eval_jaxpr/psum | solution.py:38
  754.2 24.1 %collective-permute-start.1 = (f32[512,2,256]{0,2,1:T(8,128)}, f32[512,2,256]{0,2,1:T(8,128)}, u32[]{:S(2)}, u32[]{:S(2)}) collective-permute-start(f32[512,2,256]{0,2,1:T(8,128)} %bitcast_add_fusion.3), channel_id=1, source_target_pairs={{0,2},{2,4},{4,6},{6,8},{8,10},{10,12},{12,14},{14,16},{16,18},{18... | collective-permute-start | bytes 3145736 | tf_op jit(solution)/shard_map/while/body/eval_jaxpr/ppermute | solution.py:11
  778.3 93.2 %all-reduce.5.cloned.1.call-start = ((), (), s32[]{:S(2)}) async-start(), calls=%async_computation.5 | async-start | bytes 1048576 | tf_op jit(solution)/shard_map/while/body/eval_jaxpr/psum | solution.py:38
  900.6 93.2 %all-reduce.5.cloned.1.call-start = ((), (), s32[]{:S(2)}) async-start(), calls=%async_computation.5 | async-start | bytes 1048576 | tf_op jit(solution)/shard_map/while/body/eval_jaxpr/psum | solution.py:38
  1022.8 93.2 %all-reduce.5.cloned.1.call-start = ((), (), s32[]{:S(2)}) async-start(), calls=%async_computation.5 | async-start | bytes 1048576 | tf_op jit(solution)/shard_map/while/body/eval_jaxpr/psum | solution.py:38
  1121.1 24.1 %collective-permute-start.1 = (f32[512,2,256]{0,2,1:T(8,128)}, f32[512,2,256]{0,2,1:T(8,128)}, u32[]{:S(2)}, u32[]{:S(2)}) collective-permute-start(f32[512,2,256]{0,2,1:T(8,128)} %bitcast_add_fusion.3), channel_id=1, source_target_pairs={{0,2},{2,4},{4,6},{6,8},{8,10},{10,12},{12,14},{14,16},{16,18},{18... | collective-permute-start | bytes 3145736 | tf_op jit(solution)/shard_map/while/body/eval_jaxpr/ppermute | solution.py:11
  1145.2 93.2 %all-reduce.5.cloned.1.call-start = ((), (), s32[]{:S(2)}) async-start(), calls=%async_computation.5 | async-start | bytes 1048576 | tf_op jit(solution)/shard_map/while/body/eval_jaxpr/psum | solution.py:38
  1267.4 93.2 %all-reduce.5.cloned.1.call-start = ((), (), s32[]{:S(2)}) async-start(), calls=%async_computation.5 | async-start | bytes 1048576 | tf_op jit(solution)/shard_map/while/body/eval_jaxpr/psum | solution.py:38
  1389.7 93.2 %all-reduce.5.cloned.1.call-start = ((), (), s32[]{:S(2)}) async-start(), calls=%async_computation.5 | async-start | bytes 1048576 | tf_op jit(solution)/shard_map/while/body/eval_jaxpr/psum | solution.py:38
  1488.0 24.1 %collective-permute-start.1 = (f32[512,2,256]{0,2,1:T(8,128)}, f32[512,2,256]{0,2,1:T(8,128)}, u32[]{:S(2)}, u32[]{:S(2)}) collective-permute-start(f32[512,2,256]{0,2,1:T(8,128)} %bitcast_add_fusion.3), channel_id=1, source_target_pairs={{0,2},{2,4},{4,6},{6,8},{8,10},{10,12},{12,14},{14,16},{16,18},{18... | collective-permute-start | bytes 3145736 | tf_op jit(solution)/shard_map/while/body/eval_jaxpr/ppermute | solution.py:11
  1512.1 93.2 %all-reduce.5.cloned.1.call-start = ((), (), s32[]{:S(2)}) async-start(), calls=%async_computation.5 | async-start | bytes 1048576 | tf_op jit(solution)/shard_map/while/body/eval_jaxpr/psum | solution.py:38
  1634.3 93.2 %all-reduce.5.cloned.1.call-start = ((), (), s32[]{:S(2)}) async-start(), calls=%async_computation.5 | async-start | bytes 1048576 | tf_op jit(solution)/shard_map/while/body/eval_jaxpr/psum | solution.py:38
  1756.6 93.2 %all-reduce.5.cloned.1.call-start = ((), (), s32[]{:S(2)}) async-start(), calls=%async_computation.5 | async-start | bytes 1048576 | tf_op jit(solution)/shard_map/while/body/eval_jaxpr/psum | solution.py:38
  1854.9 24.1 %collective-permute-start.1 = (f32[512,2,256]{0,2,1:T(8,128)}, f32[512,2,256]{0,2,1:T(8,128)}, u32[]{:S(2)}, u32[]{:S(2)}) collective-permute-start(f32[512,2,256]{0,2,1:T(8,128)} %bitcast_add_fusion.3), channel_id=1, source_target_pairs={{0,2},{2,4},{4,6},{6,8},{8,10},{10,12},{12,14},{14,16},{16,18},{18... | collective-permute-start | bytes 3145736 | tf_op jit(solution)/shard_map/while/body/eval_jaxpr/ppermute | solution.py:11
  1879.0 93.2 %all-reduce.5.cloned.1.call-start = ((), (), s32[]{:S(2)}) async-start(), calls=%async_computation.5 | async-start | bytes 1048576 | tf_op jit(solution)/shard_map/while/body/eval_jaxpr/psum | solution.py:38
  2001.2 89.8 %all-reduce.3.cloned.1.call-start = ((), (), s32[]{:S(2)}) async-start(), calls=%async_computation.3 | async-start | bytes 1048576 | tf_op jit(solution)/shard_map/psum | solution.py:38
  2005.0 136.4 %reduce-scatter.2.cloned.1.call-start = ((), (), s32[]{:S(2)}) async-start(), calls=%async_computation.4 | async-start | bytes 1572864 | tf_op jit(solution)/shard_map/reduce_scatter | solution.py:114
  (31 other events, 638.9 us)
Sparse Core Ops, SparseCore 0:
  179.1 80.8 all-reduce.4
  296.4 85.8 all-reduce.4
  418.8 85.7 all-reduce.4
  541.0 85.7 all-reduce.4
  663.3 85.8 all-reduce.4
  785.6 85.7 all-reduce.4
  907.9 85.7 all-reduce.4
  1030.2 85.8 all-reduce.4
  1152.5 85.7 all-reduce.4
  1274.8 85.7 all-reduce.4
  1397.1 85.8 all-reduce.4
  1519.4 85.7 all-reduce.4
  1641.7 85.7 all-reduce.4
  1764.0 85.8 all-reduce.4
  1886.3 85.7 all-reduce.4
Sparse Core Ops, SparseCore 1:
  2005.1 85.9 all-reduce.2
  2113.4 28.0 reduce-scatter.1
where the time goes:
time: 2160 us; the launch traced here: 2150 us
  waiting for transfers between devices  1640 us (76%)
  local copies, waits for them, and re-layouts  164 us (8%)
  other arithmetic  118 us (5%)
  starting transfers between devices  117 us (5%)
  matrix products  98.3 us (5%)
    psum x16, waiting for transfers between devices, block_terms(): intersection = lax.psum(partial_intersection, 'aux')  1350 us
    ppermute x31, waiting for transfers between devices, from_behind(): return lax.ppermute(x, axis, [(i, (i + by) % peers) for i in range(peers)])  174 us
    ppermute x31, starting transfers between devices, from_behind(): return lax.ppermute(x, axis, [(i, (i + by) % peers) for i in range(peers)])  103 us
    all_to_all x1, waiting for transfers between devices, shards(): lax.all_to_all(second_factors, ('occ', 'pair'), split_axis=1, concat_axis...  89.9 us
    scatter-add x16, other arithmetic, block_terms(): second_total = second_total.at[:, flat_picks, :].add(toward_second)  72.7 us
    gather x16, local copies, waits for them, and re-layouts, block_terms(): right_rows = jnp.take(second_blocks, flat_picks, axis=1)  45.8 us
  transfers between devices with their start and end apart: 50, of which 35 were waited for; matrix products, arithmetic and copies ran while one was open for 7% of the time, Pallas kernels for 0%

commit v1 on v0

v1 whole, which is shorter than its diff:
```python
import functools

import jax
import jax.numpy as jnp
from jax import lax
from jax.experimental import pallas as pl
from jax.experimental.pallas import tpu as pltpu
from jax.sharding import PartitionSpec as P

MESH = pl.DeviceIdType.MESH
F32 = jnp.float32
BF16 = jnp.bfloat16
BLK = 64
LANES = 128
NX = 4
VMEM_LIMIT = 52 * 1024 * 1024


def place():
    aux, occ, pair = lax.axis_index("aux"), lax.axis_index("occ"), lax.axis_index("pair")
    return aux, occ // 2, occ % 2, pair


def device(aux, z, core, pair):
    return {"aux": aux, "occ": z * 2 + core, "pair": pair}


def push(src, dst, send, recv, to):
    copy = pltpu.make_async_remote_copy(
        src_ref=src, dst_ref=dst, send_sem=send, recv_sem=recv, device_id=to, device_id_type=MESH
    )
    copy.start()
    return copy


def landed(ref, send, recv, to):
    pltpu.make_async_remote_copy(
        src_ref=ref, dst_ref=ref, send_sem=send, recv_sem=recv, device_id=to, device_id_type=MESH
    ).wait_recv()


def greet(peers):
    barrier = pltpu.get_barrier_semaphore()
    for peer in peers:
        pl.semaphore_signal(barrier, inc=1, device_id=peer, device_id_type=MESH)
    pl.semaphore_wait(barrier, len(peers))


def plane_peers(a, z, c, p, naux):
    return [
        device((a + da) % naux, z, c, (p + dp) % 2)
        for da in range(naux)
        for dp in range(2)
        if (da, dp) != (0, 0)
    ]


class Ring:
    def __init__(self, block, half, z, nz, c, me, sems):
        self.block, self.half, self.z, self.nz, self.c = block, half, z, nz, c
        self.me = me
        self.up_send, self.up_recv, self.dn_send, self.dn_recv, self.co_send, self.co_recv = sems
        self.up, self.dn, self.co = me(1, 0), me(-1, 0), me(0, 1)
        self.far = nz // 2
        self.sent = []

    def piece(self, way, step, core):
        origin = (self.z - way * (step + 1) + self.nz) % self.nz
        if step + 1 == self.far:
            return self.half(origin, core, 0 if way > 0 else 1)
        return self.block(origin, core)

    def start(self, source, source_halves):
        mine = self.block(self.z, self.c)
        if self.far == 1:
            raise ValueError("short ring")
        self.sent.append(push(source, mine, self.up_send.at[0], self.up_recv.at[0], self.up))
        self.sent.append(push(source, mine, self.dn_send.at[0], self.dn_recv.at[0], self.dn))
        self.sent.append(push(source, mine, self.co_send.at[0], self.co_recv.at[0], self.co))

    def step(self, step):
        for way, send, recv, to in (
            (1, self.up_send, self.up_recv, self.up),
            (-1, self.dn_send, self.dn_recv, self.dn),
        ):
            got = self.piece(way, step, self.c)
            landed(got, send.at[step], recv.at[step], to)
            if step + 1 < self.far:
                onward = got
                if step + 2 == self.far:
                    origin = (self.z - way * (step + 1) + self.nz) % self.nz
                    onward = self.half(origin, self.c, 0 if way > 0 else 1)
                self.sent.append(push(onward, onward, send.at[step + 1], recv.at[step + 1], to))
            k = 1 + 2 * step + (0 if way > 0 else 1)
            self.sent.append(push(got, got, self.co_send.at[k], self.co_recv.at[k], self.co))

    def finish(self):
        other = 1 - self.c
        landed(self.block(self.z, other), self.co_send.at[0], self.co_recv.at[0], self.co)
        for step in range(self.far):
            for way in (1, -1):
                k = 1 + 2 * step + (0 if way > 0 else 1)
                landed(self.piece(way, step, other), self.co_send.at[k], self.co_recv.at[k], self.co)
        for copy in self.sent:
            copy.wait_send()


def ring_sems(nz):
    far = nz // 2
    return [pltpu.SemaphoreType.DMA((far,))] * 4 + [pltpu.SemaphoreType.DMA((1 + 2 * far,))] * 2


def spread_kernel(
    naux, nz, second, first, sec, firstz, firsta, a_send, a_recv, b_send, b_recv, loc, *sems
):
    a, z, c, p = place()
    x, yh = a // 2, a % 2

    def me(dz, dc):
        return device(a, (z + dz + nz) % nz, (c + dc) % 2, p)

    in_plane = plane_peers(a, z, c, p, naux)
    greet(in_plane + [me(1, 0), me(-1, 0), me(0, 1)])

    locals_ = [
        pltpu.make_async_copy(first, firstz.at[:, a], loc.at[0]),
        pltpu.make_async_copy(first, firsta.at[:, z * 2 + c], loc.at[1]),
        pltpu.make_async_copy(second.at[a, :, p], sec.at[:, a * 2 + p], loc.at[2]),
    ]
    sent = []
    right = device((x + 1) % NX * 2 + yh, z, c, p)
    left = device((x + NX - 1) % NX * 2 + yh, z, c, p)
    across = device(x * 2 + (1 - yh), z, c, 1 - p)
    beside = device(a, z, c, 1 - p)
    al = (x + NX - 1) % NX * 2 + yh
    ar = (x + 1) % NX * 2 + yh
    af = (x + 2) % NX * 2 + yh
    sent.append(push(first, firstz.at[:, a], b_send.at[0], b_recv.at[0], right))
    sent.append(push(first, firstz.at[:, a], b_send.at[1], b_recv.at[1], left))
    sent.append(push(first.at[p], firstz.at[p, a], b_send.at[4], b_recv.at[4], across))
    ring = Ring(
        lambda zz, cc: firsta.at[:, zz * 2 + cc],
        lambda zz, cc, h: firsta.at[h, zz * 2 + cc],
        z, nz, c, me, sems,
    )
    ring.start(first, None)
    n = 0
    for da in range(naux):
        for dp in range(2):
            if (da, dp) != (0, 0):
                ta, tp = (a + da) % naux, (p + dp) % 2
                sent.append(
                    push(second.at[ta, :, tp], sec.at[:, a * 2 + p], a_send.at[n], a_recv.at[n],
                         device(ta, z, c, tp))
                )
                n += 1
    for copy in locals_:
        copy.start()

    landed(firstz.at[:, al], b_send.at[0], b_recv.at[0], left)
    sent.append(push(firstz.at[0, al], firstz.at[0, al], b_send.at[2], b_recv.at[2], right))
    sent.append(push(firstz.at[p, al], firstz.at[p, al], b_send.at[5], b_recv.at[5], across))
    landed(firstz.at[:, ar], b_send.at[1], b_recv.at[1], right)
    sent.append(push(firstz.at[1, ar], firstz.at[1, ar], b_send.at[3], b_recv.at[3], left))
    sent.append(push(firstz.at[p, ar], firstz.at[p, ar], b_send.at[6], b_recv.at[6], across))
    ring.step(0)

    def relay(k, slot):
        got = firstz.at[1 - p, slot // 2 * 2 + (1 - yh)]
        landed(got, b_send.at[4 + k], b_recv.at[4 + k], across)
        sent.append(push(got, got, b_send.at[8 + k], b_recv.at[8 + k], beside))

    relay(0, a)
    landed(firstz.at[0, af], b_send.at[2], b_recv.at[2], left)
    landed(firstz.at[1, af], b_send.at[3], b_recv.at[3], right)
    sent.append(push(firstz.at[p, af], firstz.at[p, af], b_send.at[7], b_recv.at[7], across))
    ring.step(1)
    relay(1, al)
    relay(2, ar)
    ring.step(2)
    relay(3, af)
    ring.step(3)
    for k, slot in enumerate((a, al, ar, af)):
        got = firstz.at[p, slot // 2 * 2 + (1 - yh)]
        landed(got, b_send.at[8 + k], b_recv.at[8 + k], beside)
    ring.finish()
    n = 0
    for da in range(naux):
        for dp in range(2):
            if (da, dp) != (0, 0):
                fa, fp = (a - da + naux) % naux, (p + dp) % 2
                landed(sec.at[:, fa * 2 + fp], a_send.at[n], a_recv.at[n], device(fa, z, c, fp))
                n += 1
    for copy in sent:
        copy.wait_send()
    for copy in locals_:
        copy.wait()


def spread(second, first, naux, nz):
    _, _, _, rows, width = second.shape
    ni, frows, _ = first.shape
    return pl.pallas_call(
        functools.partial(spread_kernel, naux, nz),
        out_shape=[
            jax.ShapeDtypeStruct((2, naux * 2, rows, width), BF16),
            jax.ShapeDtypeStruct((ni, naux, frows, width), BF16),
            jax.ShapeDtypeStruct((ni, nz * 2, frows, width), BF16),
        ],
        in_specs=[pl.BlockSpec(memory_space=pl.ANY)] * 2,
        out_specs=[pl.BlockSpec(memory_space=pl.ANY)] * 3,
        scratch_shapes=[
            pltpu.SemaphoreType.DMA((naux * 2 - 1,)),
            pltpu.SemaphoreType.DMA((naux * 2 - 1,)),
            pltpu.SemaphoreType.DMA((12,)),
            pltpu.SemaphoreType.DMA((12,)),
            pltpu.SemaphoreType.DMA((3,)),
            *ring_sems(nz),
        ],
        compiler_params=pltpu.CompilerParams(
            collective_id=1, has_side_effects=True, vmem_limit_bytes=VMEM_LIMIT
        ),
        name="spread",
    )(second, first)


def tile_of(ref, lead, block):
    return ref[(*lead, slice(None), pl.ds(pl.multiple_of(block // 2 * LANES, LANES), LANES))]


def cross_kernel(group, nb, kept, sec, first, own, other):
    i, g = pl.program_id(0), pl.program_id(1)
    lane = lax.broadcasted_iota(jnp.int32, (BLK, LANES), 1)
    for pairs in range(group // 2):
        left = first[0, :, pairs * LANES:(pairs + 1) * LANES].T
        for side, out in ((0, own), (1, other)):
            for e in range(2):
                entry = pairs * 2 + e
                at = ((side * 2 + i) * nb + g * group + entry) * 2
                b0, b1 = kept[at], kept[at + 1]
                which = kept[4 * nb * 2] if side == 0 else 1 - kept[4 * nb * 2]
                right = jnp.concatenate(
                    [tile_of(sec, (which,), b0), tile_of(sec, (which,), b1)], axis=1
                )
                prod = lax.dot_general(
                    left[e * BLK:(e + 1) * BLK], right, (((1,), (0,)), ((), ())),
                    preferred_element_type=F32,
                )
                u0, u1 = prod[:, :LANES], prod[:, LANES:]
                r0 = jnp.where(b0 % 2 == 0, u0, pltpu.roll(u0, BLK, 1))
                r1 = jnp.where(b1 % 2 == 1, u1, pltpu.roll(u1, BLK, 1))
                out[entry] = jnp.where(lane < BLK, r0, r1).astype(out.dtype)


def cross(kept, sec, first, group=8):
    _, rows, width = sec.shape
    ni = first.shape[0]
    nb = width // BLK
    groups = nb // group
    entries = ni * nb
    return pl.pallas_call(
        functools.partial(cross_kernel, group, nb),
        out_shape=[
            jax.ShapeDtypeStruct((entries, BLK, LANES), F32),
            jax.ShapeDtypeStruct((entries, BLK, LANES), BF16),
        ],
        grid_spec=pltpu.PrefetchScalarGridSpec(
            num_scalar_prefetch=1,
            grid=(ni, groups),
            in_specs=[
                pl.BlockSpec((2, rows, width), lambda i, g, kept: (0, 0, 0)),
                pl.BlockSpec((1, rows, group * BLK), lambda i, g, kept: (i, 0, g)),
            ],
            out_specs=[
                pl.BlockSpec((group, BLK, LANES), lambda i, g, kept: (i * groups + g, 0, 0)),
                pl.BlockSpec((group, BLK, LANES), lambda i, g, kept: (i * groups + g, 0, 0)),
            ],
        ),
        compiler_params=pltpu.CompilerParams(vmem_limit_bytes=VMEM_LIMIT),
        name="cross",
    )(kept, sec, first)


def amplitude_kernel(
    naux, nz, own, other, divisor, amp1, amp2,
    twin, pairsum, got, shard, d_send, d_recv, r_send, r_recv, t_send, t_recv, x_send, x_recv,
    loc, *sems
):
    a, z, c, p = place()
    size = divisor.shape[0]

    def me(dz, dc):
        return device(a, (z + dz) % nz, (c + dc) % 2, p)

    sibling = me(0, 1)
    mirror = device(z, a, c, p)
    line = [device((a + da) % naux, z, c, p) for da in range(1, naux)]
    barrier = pltpu.get_barrier_semaphore()
    peers = [sibling] + [me(dz, 0) for dz in range(1, nz)] + line
    for peer in peers:
        pl.semaphore_signal(barrier, inc=1, device_id=peer, device_id_type=MESH)

    @pl.when(a != z)
    def _():
        pl.semaphore_signal(barrier, inc=1, device_id=mirror, device_id_type=MESH)
        pl.semaphore_wait(barrier, len(peers) + 1)

    @pl.when(a == z)
    def _():
        pl.semaphore_wait(barrier, len(peers))

    def rows(t):
        return pl.ds(t * size, size)

    order = sorted(range(nz), key=lambda d: (-min(d, nz - d), d))
    sent = []
    for dz in order:
        part = rows((z + dz) % nz)
        sent.append(push(other.at[part], twin.at[part], d_send.at[dz], d_recv.at[dz], sibling))
    for dz in order:
        t = (z + dz) % nz
        landed(twin.at[rows(t)], d_send.at[dz], d_recv.at[dz], sibling)
        if dz == 0:
            continue

        def add(k, _):
            n = t * size + k
            pairsum[n] = (own[n] + twin[n].astype(F32)).astype(BF16)
            return 0

        lax.fori_loop(0, size, add, 0)
        sent.append(push(pairsum.at[rows(t)], got.at[dz], r_send.at[dz], r_recv.at[dz], me(dz, 0)))
    for dz in range(1, nz):
        landed(got.at[dz], r_send.at[dz], r_recv.at[dz], me(nz - dz, 0))

    def reduce(k, _):
        n = z * size + k
        total = own[n] + twin[n].astype(F32)
        for dz in range(1, nz):
            total = total + got[dz, k].astype(F32)
        shard[k] = (total / divisor[k]).astype(BF16)
        return 0

    lax.fori_loop(0, size, reduce, 0)

    half = size // 2
    ring = Ring(
        lambda zz, cc: amp1.at[cc, pl.ds(zz * size, size)],
        lambda zz, cc, h: amp1.at[cc, pl.ds(zz * size + h * half, half)],
        z, nz, c, lambda dz, dc: me((dz + nz) % nz, dc), sems,
    )

    @pl.when(a != z)
    def _():
        push(shard, amp2.at[rows(z)], t_send.at[0], t_recv.at[0], mirror)

    @pl.when(a == z)
    def _():
        pltpu.make_async_copy(shard, amp2.at[rows(z)], loc.at[0]).start()

    ring.start(shard, None)
    here = pltpu.make_async_copy(shard, amp1.at[c, rows(z)], loc.at[1])
    here.start()

    @pl.when(a != z)
    def _():
        landed(amp2.at[rows(a)], t_send.at[0], t_recv.at[0], mirror)

    @pl.when(a == z)
    def _():
        pltpu.make_async_copy(shard, amp2.at[rows(z)], loc.at[0]).wait()

    for k, peer in enumerate(line):
        sent.append(push(amp2.at[rows(a)], amp2.at[rows(a)], x_send.at[k], x_recv.at[k], peer))
    for step in range(nz // 2):
        ring.step(step)
    for k in range(naux - 1):
        fa = (a - (k + 1) + naux) % naux
        landed(amp2.at[rows(fa)], x_send.at[k], x_recv.at[k], device(fa, z, c, p))
    ring.finish()
    here.wait()
    for copy in sent:
        copy.wait_send()

    @pl.when(a != z)
    def _():
        pltpu.make_async_remote_copy(
            src_ref=shard, dst_ref=amp2.at[rows(z)], send_sem=t_send.at[0], recv_sem=t_recv.at[0],
            device_id=mirror, device_id_type=MESH,
        ).wait_send()


def amplitudes(own, other, divisor, naux, nz):
    entries, rows, lanes = own.shape
    size = divisor.shape[0]
    dma = pltpu.SemaphoreType.DMA
    return pl.pallas_call(
        functools.partial(amplitude_kernel, naux, nz),
        out_shape=[
            jax.ShapeDtypeStruct((2, entries, rows, lanes), BF16),
            jax.ShapeDtypeStruct((entries, rows, lanes), BF16),
        ],
        in_specs=[
            pl.BlockSpec(memory_space=pltpu.VMEM),
            pl.BlockSpec(memory_space=pl.ANY),
            pl.BlockSpec(memory_space=pltpu.VMEM),
        ],
        out_specs=[pl.BlockSpec(memory_space=pl.ANY)] * 2,
        scratch_shapes=[
            pltpu.VMEM((entries, rows, lanes), BF16),
            pltpu.VMEM((entries, rows, lanes), BF16),
            pltpu.VMEM((nz, size, rows, lanes), BF16),
            pltpu.VMEM((size, rows, lanes), BF16),
            dma((nz,)), dma((nz,)), dma((nz,)), dma((nz,)), dma((1,)), dma((1,)),
            dma((naux - 1,)), dma((naux - 1,)), dma((2,)),
            *ring_sems(nz),
        ],
        compiler_params=pltpu.CompilerParams(
            collective_id=2, has_side_effects=True, vmem_limit_bytes=VMEM_LIMIT
        ),
        name="amplitudes",
    )(own, other, divisor)


def spread_halves(amp, b0, b1):
    lane = lax.broadcasted_iota(jnp.int32, (BLK, LANES), 1) // BLK
    turned = pltpu.roll(amp, BLK, 1)
    zero = jnp.zeros_like(amp)
    t0 = jnp.where(lane == b0 % 2, jnp.where(b0 % 2 == 0, amp, turned), zero)
    t1 = jnp.where(lane == b1 % 2, jnp.where(b1 % 2 == 1, amp, turned), zero)
    return t0, t1


def toward_first_kernel(group, nb, kept, sec, amp, out):
    i, g = pl.program_id(0), pl.program_id(1)
    for pairs in range(group // 2):
        halves = []
        for e in range(2):
            entry = pairs * 2 + e
            tiles, weights = [], []
            for core in range(2):
                side = jnp.where(kept[4 * nb * 2] == core, 0, 1)
                at = ((side * 2 + i) * nb + g * group + entry) * 2
                b0, b1 = kept[at], kept[at + 1]
                tiles += [tile_of(sec, (core,), b0), tile_of(sec, (core,), b1)]
                weights += spread_halves(amp[core, entry].astype(F32), b0, b1)
            halves.append(
                lax.dot_general(
                    jnp.concatenate(tiles, axis=1),
                    jnp.concatenate(weights, axis=1).astype(BF16),
                    (((1,), (1,)), ((), ())),
                    preferred_element_type=F32,
                )
            )
        out[0, :, pairs * LANES:(pairs + 1) * LANES] = jnp.concatenate(halves, axis=1).astype(BF16)


def toward_first(kept, sec, amp, ni, group=8):
    _, rows, width = sec.shape
    nb = width // BLK
    groups = nb // group
    return pl.pallas_call(
        functools.partial(toward_first_kernel, group, nb),
        out_shape=jax.ShapeDtypeStruct((ni, rows, width), BF16),
        grid_spec=pltpu.PrefetchScalarGridSpec(
            num_scalar_prefetch=1,
            grid=(ni, groups),
            in_specs=[
                pl.BlockSpec((2, rows, width), lambda i, g, kept: (0, 0, 0)),
                pl.BlockSpec((2, group, BLK, LANES), lambda i, g, kept: (0, i * groups + g, 0, 0)),
            ],
            out_specs=pl.BlockSpec((1, rows, group * BLK), lambda i, g, kept: (i, 0, g)),
        ),
        compiler_params=pltpu.CompilerParams(vmem_limit_bytes=VMEM_LIMIT),
        name="toward_first",
    )(kept, sec, amp)


def toward_second_kernel(group, nb, kept, first, amp, out, total):
    i, g = pl.program_id(0), pl.program_id(1)

    @pl.when((i == 0) & (g == 0))
    def _():
        total[...] = jnp.zeros_like(total)

    nothing = jnp.zeros((BLK, 2 * LANES), BF16)
    for pairs in range(group // 2):
        left = first[0, :, pairs * LANES:(pairs + 1) * LANES]
        for e in range(2):
            entry = pairs * 2 + e
            at = (i * nb + g * group + entry) * 2
            b0, b1 = kept[at], kept[at + 1]
            t0, t1 = spread_halves(amp[entry].astype(F32), b0, b1)
            weights = jnp.concatenate([t0, t1], axis=1).astype(BF16)
            stack = [weights, nothing] if e == 0 else [nothing, weights]
            term = jnp.dot(left, jnp.concatenate(stack, axis=0), preferred_element_type=F32)
            for b, part in ((b0, term[:, :LANES]), (b1, term[:, LANES:])):
                at_lanes = pl.ds(pl.multiple_of(b // 2 * LANES, LANES), LANES)
                total[:, at_lanes] += part

    @pl.when((i == pl.num_programs(0) - 1) & (g == pl.num_programs(1) - 1))
    def _():
        out[...] = total[...].astype(BF16)


def toward_second(kept, first, amp, group=8):
    ni, rows, width = first.shape
    nb = width // BLK
    groups = nb // group
    return pl.pallas_call(
        functools.partial(toward_second_kernel, group, nb),
        out_shape=jax.ShapeDtypeStruct((rows, width), BF16),
        grid_spec=pltpu.PrefetchScalarGridSpec(
            num_scalar_prefetch=1,
            grid=(ni, groups),
            in_specs=[
                pl.BlockSpec((1, rows, group * BLK), lambda i, g, kept: (i, 0, g)),
                pl.BlockSpec((group, BLK, LANES), lambda i, g, kept: (i * groups + g, 0, 0)),
            ],
            out_specs=pl.BlockSpec((rows, width), lambda i, g, kept: (0, 0)),
            scratch_shapes=[pltpu.VMEM((rows, width), F32)],
        ),
        compiler_params=pltpu.CompilerParams(vmem_limit_bytes=VMEM_LIMIT),
        name="toward_second",
    )(kept, first, amp)


def gather_first_kernel(naux, nz, part, out, got, done, a_send, a_recv, z_send, z_recv, loc):
    a, z, c, p = place()
    width = out.shape[2]
    in_plane = plane_peers(a, z, c, p, naux)
    column = [(dz, dc) for dz in range(nz) for dc in range(2) if (dz, dc) != (0, 0)]

    def me(dz, dc):
        return device(a, (z + dz) % nz, (c + dc) % 2, p)

    greet(in_plane + [me(dz, dc) for dz, dc in column])
    here = pltpu.make_async_copy(part.at[p, a], got.at[0], loc.at[0])
    here.start()
    sent = []
    n = 0
    for da in range(naux):
        for dp in range(2):
            if (da, dp) != (0, 0):
                ta, tp = (a + da) % naux, (p + dp) % 2
                n += 1
                sent.append(
                    push(part.at[tp, ta], got.at[n], a_send.at[n], a_recv.at[n], device(ta, z, c, tp))
                )
    n = 0
    for da in range(naux):
        for dp in range(2):
            if (da, dp) != (0, 0):
                n += 1
                fa, fp = (a - da + naux) % naux, (p + dp) % 2
                landed(got.at[n], a_send.at[n], a_recv.at[n], device(fa, z, c, fp))
    here.wait()
    step = 2 * width

    def add(k, _):
        cols = pl.ds(pl.multiple_of(k * step, step), step)
        total = got[0, :, cols].astype(F32)
        for n in range(1, 2 * naux):
            total = total + got[n, :, cols].astype(F32)
        done[:, cols] = total.astype(BF16)
        return 0

    lax.fori_loop(0, nz, add, 0)

    def columns(to_z, to_c):
        return pl.ds(pl.multiple_of((to_z * 2 + to_c) * width, width), width)

    mine = pltpu.make_async_copy(done.at[:, columns(z, c)], out.at[z * 2 + c], loc.at[1])
    mine.start()
    for n, (dz, dc) in enumerate(column):
        tz, tc = (z + dz) % nz, (c + dc) % 2
        sent.append(
            push(done.at[:, columns(tz, tc)], out.at[z * 2 + c], z_send.at[n], z_recv.at[n],
                 device(a, tz, tc, p))
        )
    for n, (dz, dc) in enumerate(column):
        fz, fc = (z - dz + nz) % nz, (c + dc) % 2
        landed(out.at[fz * 2 + fc], z_send.at[n], z_recv.at[n], device(a, fz, fc, p))
    mine.wait()
    for copy in sent:
        copy.wait_send()


def gather_first(part, naux, nz):
    _, _, rows, width = part.shape
    dma = pltpu.SemaphoreType.DMA
    return pl.pallas_call(
        functools.partial(gather_first_kernel, naux, nz),
        out_shape=jax.ShapeDtypeStruct((nz * 2, rows, width // (nz * 2)), BF16),
        in_specs=[pl.BlockSpec(memory_space=pl.ANY)],
        out_specs=pl.BlockSpec(memory_space=pl.ANY),
        scratch_shapes=[
            pltpu.VMEM((naux * 2, rows, width), BF16),
            pltpu.VMEM((rows, width), BF16),
            dma((naux * 2,)), dma((naux * 2,)), dma((nz * 2,)), dma((nz * 2,)), dma((2,)),
        ],
        compiler_params=pltpu.CompilerParams(
            collective_id=3, has_side_effects=True, vmem_limit_bytes=VMEM_LIMIT
        ),
        name="gather_first",
    )(part)


def shards(first_factors, second_factors, first_energy, second_energy, virtual_energy, kept_blocks):
    naux, nz = lax.axis_size("aux"), lax.axis_size("occ") // 2
    a, z, c, p = place()
    rows, nj, width = second_factors.shape
    frows, ni, _ = first_factors.shape
    nb = width // BLK
    entries = ni * nb

    order = [
        (aa * 2 * nz + zz * 2 + cc, zz * 2 * nz + aa * 2 + cc)
        for aa in range(naux) for zz in range(nz) for cc in range(2)
    ]
    kept_here = kept_blocks[:, 0].reshape(entries * 2)
    kept_mine = lax.ppermute(kept_here, ("aux", "occ"), order)
    energy_mine = lax.ppermute(second_energy, ("aux", "occ"), order)
    swap = [(o, o // 2 * 2 + 1 - o % 2) for o in range(2 * nz)]
    kept_twin = lax.ppermute(kept_mine, "occ", swap)
    kept = jnp.concatenate([kept_mine, kept_twin, jnp.full((8,), c, jnp.int32)])

    size = entries // nz
    energy_blocks = virtual_energy.reshape(nb, BLK)
    picked = lax.dynamic_slice_in_dim(kept_mine, z * size * 2, size * 2, 0)
    entry = z * size + jnp.arange(size)
    left = jnp.take(energy_blocks, entry % nb, axis=0)
    right = jnp.take(energy_blocks, picked, axis=0).reshape(size, 2 * BLK)
    low = jnp.take(first_energy, entry // nb)
    divisor = left[:, :, None] + right[:, None, :] - low[:, None, None] - energy_mine[0]

    second = jnp.transpose(second_factors, (1, 0, 2)).reshape(naux, 2, 2, rows, width)
    first = jnp.transpose(first_factors, (1, 0, 2))
    sec, firstz, firsta = spread(second, first, naux, nz)
    sec = sec.reshape(2, naux * 2 * rows, width)
    firstz = firstz.reshape(ni, naux * frows, width)
    firsta = firsta.reshape(ni, nz * 2 * frows, width)

    own, other = cross(kept, sec, firstz)
    amp1, amp2 = amplitudes(own, other, divisor, naux, nz)
    part = toward_first(kept, sec, amp1, ni)
    first_density = gather_first(part.reshape(ni, naux, frows, width), naux, nz)
    second_density = toward_second(kept_here, firsta, amp2)
    return (
        first_density.reshape(nz * 2 * frows, 1, width // (nz * 2)),
        second_density.reshape(nz * 2 * frows, 1, width),
    )


def solution(mesh):
    placed = (
        P(("aux", "occ"), None, None),
        P(("aux", "occ", "pair"), None, None),
        P(),
        P(("occ", "pair")),
        P(),
        P(None, ("occ", "pair"), None, None),
    )
    return jax.shard_map(
        shards,
        mesh=mesh,
        in_specs=placed,
        out_specs=(P("aux", "pair", "occ"), P("aux", ("occ", "pair"), None)),
        check_vma=False,
    )
```

time: 2160 us -> 417 us (0.19)
  waiting for transfers between devices: 1640 us -> 0.12 us
  Pallas kernels: 0 us -> 386 us
  local copies, waits for them, and re-layouts: 164 us -> 13 us
  other arithmetic: 118 us -> 2.43 us
  starting transfers between devices: 117 us -> 13.3 us
  matrix products: 98.3 us -> 0 us
    psum x16 -> x0, waiting for transfers between devices: 1350 us -> none  [block_terms(): intersection = lax.psum(partial_intersection, 'aux')]
    pallas_call x0 -> x6, Pallas kernels: none -> 386 us  [the longest x1 115 us: spread(): pl.pallas_call(functools.partial(spread_kernel, naux, nz), out_shape=[jax...]
    ppermute x31 -> x3, waiting for transfers between devices: 174 us -> 0.12 us  [the longest x1 0.11 us: shards(): kept_twin = lax.ppermute(kept_mine, 'occ', swap)]
    all_to_all x2 -> x0, waiting for transfers between devices: 101 us -> none  [the longest x1 89.9 us: shards(): lax.all_to_all(second_factors, ('occ', 'pair'), split_axis=1, concat_axis...]
    dot_general x48 -> x0, matrix products: 98.3 us -> none  [the longest x16 41.7 us: block_terms(): jnp.einsum('nab,pnb->pna', amplitude, right_rows, preferred_element_type=...]
    ppermute x31 -> x3, starting transfers between devices: 103 us -> 13.3 us  [the longest x1 8.99 us: shards(): energy_mine = lax.ppermute(second_energy, ('aux', 'occ'), order)]
    scatter-add x16 -> x0, other arithmetic: 72.7 us -> none  [block_terms(): second_total = second_total.at[:, flat_picks, :].add(toward_second)]
    gather x32 -> x4, local copies, waits for them, and re-layouts: 54.9 us -> 2.52 us  [the longest x1 1.31 us: shards(): low = jnp.take(first_energy, entry // nb)]
  transfers between devices with their start and end apart: 50 -> 3, of which waited for: 35 -> 1; matrix products, arithmetic and copies ran while one was open for 7% -> 4% of each run, Pallas kernels for 0% -> 28%
where the time goes in v1:
time: 417 us; the launch traced here: 416 us
  Pallas kernels  386 us (93%)
  starting transfers between devices  13.3 us (3%)
  local copies, waits for them, and re-layouts  13 us (3%)
    pallas_call x1, Pallas kernels, spread(): pl.pallas_call(functools.partial(spread_kernel, naux, nz), out_shape=[jax...  115 us
    pallas_call x1, Pallas kernels, amplitudes(): pl.pallas_call(functools.partial(amplitude_kernel, naux, nz), out_shape=[...  114 us
    pallas_call x1, Pallas kernels, gather_first(): pl.pallas_call(functools.partial(gather_first_kernel, naux, nz), out_shap...  90.4 us
    pallas_call x1, Pallas kernels, toward_second(): pl.pallas_call(functools.partial(toward_second_kernel, group, nb), out_sh...  29.7 us
    pallas_call x1, Pallas kernels, toward_first(): pl.pallas_call(functools.partial(toward_first_kernel, group, nb), out_sha...  19.2 us
    pallas_call x1, Pallas kernels, cross(): pl.pallas_call(functools.partial(cross_kernel, group, nb), out_shape=[jax...  18.6 us
    ppermute x1, starting transfers between devices, shards(): energy_mine = lax.ppermute(second_energy, ('aux', 'occ'), order)  8.99 us
  transfers between devices with their start and end apart: 3, of which 1 were waited for; matrix products, arithmetic and copies ran while one was open for 4% of the time, Pallas kernels for 28%

profile of v1, /device:TPU:29, one launch (start us, length us, event | category | flops | bytes accessed | tf_op | source)
XLA Modules:
  0.0 416.0 jit_solution(4644467014248234809)
XLA Ops:
  0.6 9.0 %collective-permute-start.2 = (f32[1]{0:T(128)}, f32[1]{0:T(128)}, u32[]{:S(2)}, u32[]{:S(2)}) collective-permute-start(f32[1]{0:T(128)} %param.9), channel_id=1, source_target_pairs={{0,0},{2,2},{4,32},{6,34},{8,64},{10,66},{12,96},{14,98},{16,128},... | collective-permute-start | bytes 20 | tf_op jit(solution)/shard_map/ppermute | solution.py:623
  9.6 0.8 copy.10
  10.4 0.1 reshape_squeeze.3.kept
  10.6 4.1 collective-permute-start
  14.7 1.3 fusion.2
  16.0 0.8 reshape.194
  16.8 0.6 gather_fusion
  17.5 1.3 and_select_fusion.1
  18.8 1.3 copy.14
  20.1 6.5 %copy.11 = bf16[32,16,4096]{2,1,0:T(8,128)(2,1)} copy(bf16[32,16,4096]{2,0,1:T(8,128)(2,1)} %bitcast.31) | data formatting | bytes 8388608 | tf_op jit(solution)/shard_map/transpose | solution.py:637
  26.6 114.9 %spread.1 = (bf16[2,16,16,4096]{3,2,1,0:T(8,128)(2,1)}, bf16[2,8,32,4096]{3,2,1,0:T(8,128)(2,1)}, bf16[2,16,32,4096]{3,2,1,0:T(8,128)(2,1)}) custom-call(bf16[8,2,2,16,4096]{4,3,2,1,0:T(8,128)(2,1)} %bitcast.26, bf16[2,32,4096]{2,1,0:T(8,128)(2,1)S(1)} %bitcast.24), custom_call_target="tpu_custom_call" | custom-call | tf_op jit(solution)/shard_map/spread/pallas_call | solution.py:203
  141.5 0.1 compare_and_fusion
  141.6 0.1 broadcast_in_dim.36
  141.7 0.6 gather_fusion.1
  142.4 0.1 broadcast_in_dim.38
  142.5 0.2 collective-permute-start.1
  142.7 0.9 subtract_subtract_fusion.divisor
  143.6 0.1 collective-permute-done.1
  143.8 18.6 %cross.1 = (f32[128,64,128]{2,1,0:T(8,128)}, bf16[128,64,128]{2,1,0:T(8,128)(2,1)}) custom-call(s32[520]{0:T(1024)S(1)} %pad_add_fusion.kept, bf16[2,256,4096]{2,1,0:T(8,128)(2,1)} %bitcast.28, bf16[2,256,4096]{2,1,0:T(8,128)(2,1)} %bitcast.32), custom_call_target="tpu_custom_call" | custom-call | tf_op jit(solution)/shard_map/cross/pallas_call | solution.py:261
  162.4 113.6 %amplitudes.1 = (bf16[2,128,64,128]{3,2,1,0:T(8,128)(2,1)}, bf16[128,64,128]{2,1,0:T(8,128)(2,1)}) custom-call(f32[128,64,128]{2,1,0:T(8,128)} %get-tuple-element.11.own, bf16[128,64,128]{2,1,0:T(8,128)(2,1)} %get-tuple-element.12.other, f32[16,64,128]{2,1,0:T(8,128)S(1)} %subtract_subtract_fusion.divisor), custom_call_target="tpu_custom_call" | custom-call | tf_op jit(solution)/shard_map/amplitudes/pallas_call | solution.py:397
  276.0 19.2 %toward_first.1 = bf16[2,256,4096]{2,1,0:T(8,128)(2,1)} custom-call(s32[520]{0:T(1024)S(1)} %pad_add_fusion.kept, bf16[2,256,4096]{2,1,0:T(8,128)(2,1)} %bitcast.29, bf16[2,128,64,128]{3,2,1,0:T(8,128)(2,1)} %get-tuple-element.13.amp), custom_call_target="tpu_custom_call" | custom-call | tf_op jit(solution)/shard_map/toward_first/pallas_call | solution.py:462
  295.2 90.4 %gather_first.1 = bf16[16,32,256]{2,1,0:T(8,128)(2,1)S(1)} custom-call(bf16[2,8,32,4096]{3,2,1,0:T(8,128)(2,1)} %bitcast.27), custom_call_target="tpu_custom_call" | custom-call | tf_op jit(solution)/shard_map/gather_first/pallas_call | solution.py:592
  385.6 29.7 %toward_second.1 = bf16[512,4096]{1,0:T(8,128)(2,1)} custom-call(s32[256]{0:T(256)S(1)} %reshape_squeeze.3.kept, bf16[2,512,4096]{2,1,0:T(8,128)(2,1)} %bitcast.30, bf16[128,64,128]{2,1,0:T(8,128)(2,1)} %get-tuple-element.15.amp), custom_call_target="tpu_custom_call" | custom-call | tf_op jit(solution)/shard_map/toward_second/pallas_call | solution.py:510
  415.2 0.7 copy.16
  (12 shorter events, 0.3 us)
Async XLA Ops:
  0.6 142.1 %collective-permute-start.2 = (f32[1]{0:T(128)}, f32[1]{0:T(128)}, u32[]{:S(2)}, u32[]{:S(2)}) collective-permute-start(f32[1]{0:T(128)} %param.9), channel_id=1, source_target_pairs={{0,0},{2,2},{4,32},{6,34},{8,64},{10,66},{12,96},{14,98},{16,128},... | collective-permute-start | bytes 20 | tf_op jit(solution)/shard_map/ppermute | solution.py:623
  10.6 131.0 %collective-permute-start = (s32[256]{0:T(256)S(1)}, s32[256]{0:T(256)S(1)}, u32[]{:S(2)}, u32[]{:S(2)}) collective-permute-start(s32[256]{0:T(256)S(1)} %reshape_squeeze.3.kept), channel_id=1, source_target_pairs={{0,0},{2,2},{4,32},{6,34},{8,64},{10,66},{12,96},{14,98},{16,128},... | collective-permute-start | bytes 3080 | tf_op jit(solution)/shard_map/ppermute | solution.py:622
  142.5 1.2 collective-permute-start.1

commit v2 on v1

--- a/solution.py
+++ b/solution.py
@@ -13,6 +13,10 @@
 BLK = 64
 LANES = 128
 NX = 4
+ORDER = (
+    (1, 0), (0, 1), (3, 0), (0, 3), (1, 1), (3, 3), (1, 3), (3, 1),
+    (2, 0), (0, 2), (2, 1), (1, 2), (2, 3), (3, 2), (2, 2),
+)
 VMEM_LIMIT = 52 * 1024 * 1024
 
 
@@ -144,26 +148,37 @@
         z, nz, c, me, sems,
     )
     ring.start(first, None)
-    n = 0
-    for da in range(naux):
-        for dp in range(2):
-            if (da, dp) != (0, 0):
-                ta, tp = (a + da) % naux, (p + dp) % 2
-                sent.append(
-                    push(second.at[ta, :, tp], sec.at[:, a * 2 + p], a_send.at[n], a_recv.at[n],
-                         device(ta, z, c, tp))
-                )
-                n += 1
+    y = yh * 2 + p
+    batches = [4, 2, 3, 2, 2, 2]
+
+    def plane(dx, dy):
+        ty = (y + dy) % 4
+        return (x + dx) % NX * 2 + ty // 2, ty % 2
+
+    def send_some():
+        for _ in range(batches.pop(0) if batches else 0):
+            n = len(second_sent)
+            ta, tp = plane(*ORDER[n])
+            second_sent.append(
+                push(second.at[ta, :, tp], sec.at[:, a * 2 + p], a_send.at[n], a_recv.at[n],
+                     device(ta, z, c, tp))
+            )
+
+    second_sent = []
+    send_some()
     for copy in locals_:
         copy.start()
 
     landed(firstz.at[:, al], b_send.at[0], b_recv.at[0], left)
     sent.append(push(firstz.at[0, al], firstz.at[0, al], b_send.at[2], b_recv.at[2], right))
     sent.append(push(firstz.at[p, al], firstz.at[p, al], b_send.at[5], b_recv.at[5], across))
+    send_some()
     landed(firstz.at[:, ar], b_send.at[1], b_recv.at[1], right)
     sent.append(push(firstz.at[1, ar], firstz.at[1, ar], b_send.at[3], b_recv.at[3], left))
     sent.append(push(firstz.at[p, ar], firstz.at[p, ar], b_send.at[6], b_recv.at[6], across))
+    send_some()
     ring.step(0)
+    send_some()
 
     def relay(k, slot):
         got = firstz.at[1 - p, slot // 2 * 2 + (1 - yh)]
@@ -171,9 +186,11 @@
         sent.append(push(got, got, b_send.at[8 + k], b_recv.at[8 + k], beside))
 
     relay(0, a)
+    send_some()
     landed(firstz.at[0, af], b_send.at[2], b_recv.at[2], left)
     landed(firstz.at[1, af], b_send.at[3], b_recv.at[3], right)
     sent.append(push(firstz.at[p, af], firstz.at[p, af], b_send.at[7], b_recv.at[7], across))
+    send_some()
     ring.step(1)
     relay(1, al)
     relay(2, ar)
@@ -184,13 +201,11 @@
         got = firstz.at[p, slot // 2 * 2 + (1 - yh)]
         landed(got, b_send.at[8 + k], b_recv.at[8 + k], beside)
     ring.finish()
-    n = 0
-    for da in range(naux):
-        for dp in range(2):
-            if (da, dp) != (0, 0):
-                fa, fp = (a - da + naux) % naux, (p + dp) % 2
-                landed(sec.at[:, fa * 2 + fp], a_send.at[n], a_recv.at[n], device(fa, z, c, fp))
-                n += 1
+    for n, (dx, dy) in enumerate(ORDER):
+        fa, fp = plane(NX - dx, 4 - dy)
+        landed(sec.at[:, fa * 2 + fp], a_send.at[n], a_recv.at[n], device(fa, z, c, fp))
+    for copy in second_sent:
+        copy.wait_send()
     for copy in sent:
         copy.wait_send()
     for copy in locals_:
@@ -283,8 +298,7 @@
 
 def amplitude_kernel(
     naux, nz, own, other, divisor, amp1, amp2,
-    twin, pairsum, got, shard, d_send, d_recv, r_send, r_recv, t_send, t_recv, x_send, x_recv,
-    loc, *sems
+    twin, outgoing, got, shard, d_send, d_recv, r_send, r_recv, t_send, t_recv, loc, *sems
 ):
     a, z, c, p = place()
     size = divisor.shape[0]
@@ -294,9 +308,8 @@
 
     sibling = me(0, 1)
     mirror = device(z, a, c, p)
-    line = [device((a + da) % naux, z, c, p) for da in range(1, naux)]
     barrier = pltpu.get_barrier_semaphore()
-    peers = [sibling] + [me(dz, 0) for dz in range(1, nz)] + line
+    peers = [sibling, me(1, 0), me(nz - 1, 0)]
     for peer in peers:
         pl.semaphore_signal(barrier, inc=1, device_id=peer, device_id_type=MESH)
 
@@ -312,38 +325,63 @@
     def rows(t):
         return pl.ds(t * size, size)
 
+    far, half = nz // 2, size // 2
     order = sorted(range(nz), key=lambda d: (-min(d, nz - d), d))
     sent = []
     for dz in order:
         part = rows((z + dz) % nz)
         sent.append(push(other.at[part], twin.at[part], d_send.at[dz], d_recv.at[dz], sibling))
-    for dz in order:
-        t = (z + dz) % nz
-        landed(twin.at[rows(t)], d_send.at[dz], d_recv.at[dz], sibling)
-        if dz == 0:
-            continue
-
-        def add(k, _):
-            n = t * size + k
-            pairsum[n] = (own[n] + twin[n].astype(F32)).astype(BF16)
-            return 0
-
-        lax.fori_loop(0, size, add, 0)
-        sent.append(push(pairsum.at[rows(t)], got.at[dz], r_send.at[dz], r_recv.at[dz], me(dz, 0)))
-    for dz in range(1, nz):
-        landed(got.at[dz], r_send.at[dz], r_recv.at[dz], me(nz - dz, 0))
+    ways = ((1, 0, me(1, 0)), (-1, 1, me(nz - 1, 0)))
+    for step in range(far):
+        for way, w, to in ways:
+            dz = way * (far - step) % nz
+            t = (z + dz) % nz
+            if step or w == 0:
+                landed(twin.at[rows(t)], d_send.at[dz], d_recv.at[dz], sibling)
+            first_row = w * half if step == 0 else 0
+            count = half if step == 0 else size
+            if step:
+                before = pl.ds(w * half, half) if step == 1 else pl.ds(0, size)
+                come = got.at[w, step - 1, before]
+                landed(come, r_send.at[w, step - 1], r_recv.at[w, step - 1], to)
+
+            def add(k, _):
+                n = t * size + k
+                total = own[n] + twin[n].astype(F32)
+                outgoing[w, step, k] = total.astype(BF16)
+                return 0
+
+            def add_got(k, _):
+                n = t * size + k
+                total = own[n] + twin[n].astype(F32) + got[w, step - 1, k].astype(F32)
+                outgoing[w, step, k] = total.astype(BF16)
+                return 0
+
+            if step == 0:
+                lax.fori_loop(first_row, first_row + count, add, 0)
+            elif step == 1:
+                lax.fori_loop(w * half, w * half + half, add_got, 0)
+                lax.fori_loop((1 - w) * half, (1 - w) * half + half, add, 0)
+            else:
+                lax.fori_loop(0, size, add_got, 0)
+            span = pl.ds(first_row, count)
+            sent.append(
+                push(outgoing.at[w, step, span], got.at[w, step, span],
+                     r_send.at[w, step], r_recv.at[w, step], to)
+            )
+    landed(twin.at[rows(z)], d_send.at[0], d_recv.at[0], sibling)
+    for way, w, to in ways:
+        landed(got.at[w, far - 1], r_send.at[w, far - 1], r_recv.at[w, far - 1], to)
 
     def reduce(k, _):
         n = z * size + k
         total = own[n] + twin[n].astype(F32)
-        for dz in range(1, nz):
-            total = total + got[dz, k].astype(F32)
+        total = total + got[0, far - 1, k].astype(F32) + got[1, far - 1, k].astype(F32)
         shard[k] = (total / divisor[k]).astype(BF16)
         return 0
 
     lax.fori_loop(0, size, reduce, 0)
 
-    half = size // 2
     ring = Ring(
         lambda zz, cc: amp1.at[cc, pl.ds(zz * size, size)],
         lambda zz, cc, h: amp1.at[cc, pl.ds(zz * size + h * half, half)],
@@ -352,32 +390,28 @@
 
     @pl.when(a != z)
     def _():
-        push(shard, amp2.at[rows(z)], t_send.at[0], t_recv.at[0], mirror)
+        push(shard, amp2, t_send.at[0], t_recv.at[0], mirror)
 
     @pl.when(a == z)
     def _():
-        pltpu.make_async_copy(shard, amp2.at[rows(z)], loc.at[0]).start()
+        pltpu.make_async_copy(shard, amp2, loc.at[0]).start()
 
     ring.start(shard, None)
     here = pltpu.make_async_copy(shard, amp1.at[c, rows(z)], loc.at[1])
     here.start()
 
-    @pl.when(a != z)
-    def _():
-        landed(amp2.at[rows(a)], t_send.at[0], t_recv.at[0], mirror)
-
-    @pl.when(a == z)
-    def _():
-        pltpu.make_async_copy(shard, amp2.at[rows(z)], loc.at[0]).wait()
-
-    for k, peer in enumerate(line):
-        sent.append(push(amp2.at[rows(a)], amp2.at[rows(a)], x_send.at[k], x_recv.at[k], peer))
     for step in range(nz // 2):
         ring.step(step)
-    for k in range(naux - 1):
-        fa = (a - (k + 1) + naux) % naux
-        landed(amp2.at[rows(fa)], x_send.at[k], x_recv.at[k], device(fa, z, c, p))
     ring.finish()
+
+    @pl.when(a != z)
+    def _():
+        landed(amp2, t_send.at[0], t_recv.at[0], mirror)
+
+    @pl.when(a == z)
+    def _():
+        pltpu.make_async_copy(shard, amp2, loc.at[0]).wait()
+
     here.wait()
     for copy in sent:
         copy.wait_send()
@@ -385,7 +419,7 @@
     @pl.when(a != z)
     def _():
         pltpu.make_async_remote_copy(
-            src_ref=shard, dst_ref=amp2.at[rows(z)], send_sem=t_send.at[0], recv_sem=t_recv.at[0],
+            src_ref=shard, dst_ref=amp2, send_sem=t_send.at[0], recv_sem=t_recv.at[0],
             device_id=mirror, device_id_type=MESH,
         ).wait_send()
 
@@ -398,7 +432,7 @@
         functools.partial(amplitude_kernel, naux, nz),
         out_shape=[
             jax.ShapeDtypeStruct((2, entries, rows, lanes), BF16),
-            jax.ShapeDtypeStruct((entries, rows, lanes), BF16),
+            jax.ShapeDtypeStruct((size, rows, lanes), BF16),
         ],
         in_specs=[
             pl.BlockSpec(memory_space=pltpu.VMEM),
@@ -408,11 +442,11 @@
         out_specs=[pl.BlockSpec(memory_space=pl.ANY)] * 2,
         scratch_shapes=[
             pltpu.VMEM((entries, rows, lanes), BF16),
-            pltpu.VMEM((entries, rows, lanes), BF16),
-            pltpu.VMEM((nz, size, rows, lanes), BF16),
+            pltpu.VMEM((2, nz // 2, size, rows, lanes), BF16),
+            pltpu.VMEM((2, nz // 2, size, rows, lanes), BF16),
             pltpu.VMEM((size, rows, lanes), BF16),
-            dma((nz,)), dma((nz,)), dma((nz,)), dma((nz,)), dma((1,)), dma((1,)),
-            dma((naux - 1,)), dma((naux - 1,)), dma((2,)),
+            dma((nz,)), dma((nz,)), dma((2, nz // 2)), dma((2, nz // 2)), dma((1,)), dma((1,)),
+            dma((2,)),
             *ring_sems(nz),
         ],
         compiler_params=pltpu.CompilerParams(
@@ -433,6 +467,7 @@
 
 def toward_first_kernel(group, nb, kept, sec, amp, out):
     i, g = pl.program_id(0), pl.program_id(1)
+    naux, _, frows, _ = out.shape
     for pairs in range(group // 2):
         halves = []
         for e in range(2):
@@ -452,16 +487,17 @@
                     preferred_element_type=F32,
                 )
             )
-        out[0, :, pairs * LANES:(pairs + 1) * LANES] = jnp.concatenate(halves, axis=1).astype(BF16)
-
-
-def toward_first(kept, sec, amp, ni, group=8):
+        both = jnp.concatenate(halves, axis=1).astype(BF16)
+        out[:, 0, :, pairs * LANES:(pairs + 1) * LANES] = both.reshape(naux, frows, LANES)
+
+
+def toward_first(kept, sec, amp, ni, naux, group=8):
     _, rows, width = sec.shape
     nb = width // BLK
     groups = nb // group
     return pl.pallas_call(
         functools.partial(toward_first_kernel, group, nb),
-        out_shape=jax.ShapeDtypeStruct((ni, rows, width), BF16),
+        out_shape=jax.ShapeDtypeStruct((naux, ni, rows // naux, width), BF16),
         grid_spec=pltpu.PrefetchScalarGridSpec(
             num_scalar_prefetch=1,
             grid=(ni, groups),
@@ -469,14 +505,20 @@
                 pl.BlockSpec((2, rows, width), lambda i, g, kept: (0, 0, 0)),
                 pl.BlockSpec((2, group, BLK, LANES), lambda i, g, kept: (0, i * groups + g, 0, 0)),
             ],
-            out_specs=pl.BlockSpec((1, rows, group * BLK), lambda i, g, kept: (i, 0, g)),
+            out_specs=pl.BlockSpec(
+                (naux, 1, rows // naux, group * BLK), lambda i, g, kept: (0, i, 0, g)
+            ),
         ),
         compiler_params=pltpu.CompilerParams(vmem_limit_bytes=VMEM_LIMIT),
+        cost_estimate=pl.CostEstimate(
+            flops=ni * nb * BLK * rows * 4 * LANES * 4, bytes_accessed=24 << 20, transcendentals=0
+        ),
         name="toward_first",
     )(kept, sec, amp)
 
 
-def toward_second_kernel(group, nb, kept, first, amp, out, total):
+def toward_second_kernel(group, nb, kept, first, amp, *rest):
+    out, total = rest[-2:]
     i, g = pl.program_id(0), pl.program_id(1)
 
     @pl.when((i == 0) & (g == 0))
@@ -503,107 +545,36 @@
         out[...] = total[...].astype(BF16)
 
 
-def toward_second(kept, first, amp, group=8):
+def toward_second(kept, first, amp, height, place_of, before, group=8):
     ni, rows, width = first.shape
     nb = width // BLK
     groups = nb // group
+    in_specs = [
+        pl.BlockSpec((1, height, group * BLK), lambda i, g, kept: (i, place_of, g)),
+        pl.BlockSpec((group, BLK, LANES), lambda i, g, kept: (i * groups + g, 0, 0)),
+    ]
+    operands = [kept, first, amp]
+    if before is not None:
+        in_specs.append(pl.BlockSpec(memory_space=pl.ANY))
+        operands.append(before)
     return pl.pallas_call(
         functools.partial(toward_second_kernel, group, nb),
         out_shape=jax.ShapeDtypeStruct((rows, width), BF16),
         grid_spec=pltpu.PrefetchScalarGridSpec(
             num_scalar_prefetch=1,
             grid=(ni, groups),
-            in_specs=[
-                pl.BlockSpec((1, rows, group * BLK), lambda i, g, kept: (i, 0, g)),
-                pl.BlockSpec((group, BLK, LANES), lambda i, g, kept: (i * groups + g, 0, 0)),
-            ],
-            out_specs=pl.BlockSpec((rows, width), lambda i, g, kept: (0, 0)),
-            scratch_shapes=[pltpu.VMEM((rows, width), F32)],
+            in_specs=in_specs,
+            out_specs=pl.BlockSpec((height, width), lambda i, g, kept: (place_of, 0)),
+            scratch_shapes=[pltpu.VMEM((height, width), F32)],
         ),
+        input_output_aliases={} if before is None else {3: 0},
         compiler_params=pltpu.CompilerParams(vmem_limit_bytes=VMEM_LIMIT),
+        cost_estimate=pl.CostEstimate(
+            flops=ni * nb * BLK * height * 4 * LANES * 4,
+            bytes_accessed=height << 18, transcendentals=0
+        ),
         name="toward_second",
-    )(kept, first, amp)
-
-
-def gather_first_kernel(naux, nz, part, out, got, done, a_send, a_recv, z_send, z_recv, loc):
-    a, z, c, p = place()
-    width = out.shape[2]
-    in_plane = plane_peers(a, z, c, p, naux)
-    column = [(dz, dc) for dz in range(nz) for dc in range(2) if (dz, dc) != (0, 0)]
-
-    def me(dz, dc):
-        return device(a, (z + dz) % nz, (c + dc) % 2, p)
-
-    greet(in_plane + [me(dz, dc) for dz, dc in column])
-    here = pltpu.make_async_copy(part.at[p, a], got.at[0], loc.at[0])
-    here.start()
-    sent = []
-    n = 0
-    for da in range(naux):
-        for dp in range(2):
-            if (da, dp) != (0, 0):
-                ta, tp = (a + da) % naux, (p + dp) % 2
-                n += 1
-                sent.append(
-                    push(part.at[tp, ta], got.at[n], a_send.at[n], a_recv.at[n], device(ta, z, c, tp))
-                )
-    n = 0
-    for da in range(naux):
-        for dp in range(2):
-            if (da, dp) != (0, 0):
-                n += 1
-                fa, fp = (a - da + naux) % naux, (p + dp) % 2
-                landed(got.at[n], a_send.at[n], a_recv.at[n], device(fa, z, c, fp))
-    here.wait()
-    step = 2 * width
-
-    def add(k, _):
-        cols = pl.ds(pl.multiple_of(k * step, step), step)
-        total = got[0, :, cols].astype(F32)
-        for n in range(1, 2 * naux):
-            total = total + got[n, :, cols].astype(F32)
-        done[:, cols] = total.astype(BF16)
-        return 0
-
-    lax.fori_loop(0, nz, add, 0)
-
-    def columns(to_z, to_c):
-        return pl.ds(pl.multiple_of((to_z * 2 + to_c) * width, width), width)
-
-    mine = pltpu.make_async_copy(done.at[:, columns(z, c)], out.at[z * 2 + c], loc.at[1])
-    mine.start()
-    for n, (dz, dc) in enumerate(column):
-        tz, tc = (z + dz) % nz, (c + dc) % 2
-        sent.append(
-            push(done.at[:, columns(tz, tc)], out.at[z * 2 + c], z_send.at[n], z_recv.at[n],
-                 device(a, tz, tc, p))
-        )
-    for n, (dz, dc) in enumerate(column):
-        fz, fc = (z - dz + nz) % nz, (c + dc) % 2
-        landed(out.at[fz * 2 + fc], z_send.at[n], z_recv.at[n], device(a, fz, fc, p))
-    mine.wait()
-    for copy in sent:
-        copy.wait_send()
-
-
-def gather_first(part, naux, nz):
-    _, _, rows, width = part.shape
-    dma = pltpu.SemaphoreType.DMA
-    return pl.pallas_call(
-        functools.partial(gather_first_kernel, naux, nz),
-        out_shape=jax.ShapeDtypeStruct((nz * 2, rows, width // (nz * 2)), BF16),
-        in_specs=[pl.BlockSpec(memory_space=pl.ANY)],
-        out_specs=pl.BlockSpec(memory_space=pl.ANY),
-        scratch_shapes=[
-            pltpu.VMEM((naux * 2, rows, width), BF16),
-            pltpu.VMEM((rows, width), BF16),
-            dma((naux * 2,)), dma((naux * 2,)), dma((nz * 2,)), dma((nz * 2,)), dma((2,)),
-        ],
-        compiler_params=pltpu.CompilerParams(
-            collective_id=3, has_side_effects=True, vmem_limit_bytes=VMEM_LIMIT
-        ),
-        name="gather_first",
-    )(part)
+    )(*operands)
 
 
 def shards(first_factors, second_factors, first_energy, second_energy, virtual_energy, kept_blocks):
@@ -643,9 +614,19 @@
 
     own, other = cross(kept, sec, firstz)
     amp1, amp2 = amplitudes(own, other, divisor, naux, nz)
-    part = toward_first(kept, sec, amp1, ni)
-    first_density = gather_first(part.reshape(ni, naux, frows, width), naux, nz)
-    second_density = toward_second(kept_here, firsta, amp2)
+    amp2 = jnp.broadcast_to(amp2[None], (naux, *amp2.shape))
+    amp2 = lax.all_to_all(amp2, "aux", split_axis=0, concat_axis=0, tiled=True)
+    amp2 = amp2.reshape(entries, BLK, LANES)
+
+    part = toward_first(kept, sec, amp1, ni, naux).reshape(naux * ni, frows, width)
+    amp2, part = lax.optimization_barrier((amp2, part))
+    terms = lax.all_to_all(part, ("aux", "pair"), split_axis=0, concat_axis=0, tiled=True)
+    most = nz * frows * 3 // 2
+    second_density = toward_second(kept_here, firsta, amp2, most, 0, None)
+    terms, second_density = lax.optimization_barrier((terms, second_density))
+    done = jnp.sum(terms.astype(F32), axis=0).astype(BF16)
+    first_density = lax.all_to_all(done, "occ", split_axis=1, concat_axis=0, tiled=True)
+    second_density = toward_second(kept_here, firsta, amp2, most // 3, 3, second_density)
     return (
         first_density.reshape(nz * 2 * frows, 1, width // (nz * 2)),
         second_density.reshape(nz * 2 * frows, 1, width),

time: 417 us -> 352 us (0.84)
  Pallas kernels: 386 us -> 234 us
  waiting for transfers between devices: 0.12 us -> 46.5 us
  starting transfers between devices: 13.3 us -> 47 us
    pallas_call x1 -> x0, Pallas kernels: 90.4 us -> none  [gather_first(): pl.pallas_call(functools.partial(gather_first_kernel, naux, nz), out_shap...]
    all_to_all x0 -> x3, waiting for transfers between devices: none -> 46.5 us  [the longest x1 38.8 us: shards(): lax.all_to_all(part, ('aux', 'pair'), split_axis=0, concat_axis=0, tiled=...]
    pallas_call x1, Pallas kernels: 115 us -> 79.8 us  [spread(): pl.pallas_call(functools.partial(spread_kernel, naux, nz), out_shape=[jax...]
    pallas_call x1, Pallas kernels: 114 us -> 78.9 us  [amplitudes(): pl.pallas_call(functools.partial(amplitude_kernel, naux, nz), out_shape=[...]
    all_to_all x0 -> x3, starting transfers between devices: none -> 31.5 us  [the longest x1 14.7 us: shards(): amp2 = lax.all_to_all(amp2, 'aux', split_axis=0, concat_axis=0, tiled=True)]
    pallas_call x1 -> x2, Pallas kernels: 29.7 us -> 37.2 us  [toward_second(): pl.pallas_call(functools.partial(toward_second_kernel, group, nb), out_sh...]
  transfers between devices with their start and end apart: 3 -> 6, of which waited for: 1 -> 2; matrix products, arithmetic and copies ran while one was open for 4% -> 4% of each run, Pallas kernels for 28% -> 39%
where the time goes in v2:
time: 352 us; the launch traced here: 350 us
  Pallas kernels  234 us (66%)
  starting transfers between devices  47 us (13%)
  waiting for transfers between devices  46.5 us (13%)
  local copies, waits for them, and re-layouts  16.9 us (5%)
  other arithmetic  5.35 us (2%)
    pallas_call x1, Pallas kernels, spread(): pl.pallas_call(functools.partial(spread_kernel, naux, nz), out_shape=[jax...  79.8 us
    pallas_call x1, Pallas kernels, amplitudes(): pl.pallas_call(functools.partial(amplitude_kernel, naux, nz), out_shape=[...  78.9 us
    all_to_all x1, waiting for transfers between devices, shards(): lax.all_to_all(part, ('aux', 'pair'), split_axis=0, concat_axis=0, tiled=...  38.8 us
    pallas_call x2, Pallas kernels, toward_second(): pl.pallas_call(functools.partial(toward_second_kernel, group, nb), out_sh...  37.2 us
    pallas_call x1, Pallas kernels, toward_first(): pl.pallas_call(functools.partial(toward_first_kernel, group, nb), out_sha...  19.2 us
    pallas_call x1, Pallas kernels, cross(): pl.pallas_call(functools.partial(cross_kernel, group, nb), out_shape=[jax...  18.6 us
    all_to_all x1, starting transfers between devices, shards(): amp2 = lax.all_to_all(amp2, 'aux', split_axis=0, concat_axis=0, tiled=True)  14.7 us
    all_to_all x1, starting transfers between devices, shards(): lax.all_to_all(part, ('aux', 'pair'), split_axis=0, concat_axis=0, tiled=...  9.17 us
  transfers between devices with their start and end apart: 6, of which 2 were waited for; matrix products, arithmetic and copies ran while one was open for 4% of the time, Pallas kernels for 39%

profile of v2, /device:TPU:29, one launch (start us, length us, event | category | flops | bytes accessed | tf_op | source)
XLA Modules:
  0.0 350.3 jit_solution(7291984401567396730)
XLA Ops:
  0.6 9.0 %collective-permute-start.2 = (f32[1]{0:T(128)}, f32[1]{0:T(128)}, u32[]{:S(2)}, u32[]{:S(2)}) collective-permute-start(f32[1]{0:T(128)} %param.9), channel_id=1, source_target_pairs={{0,0},{2,2},{4,32},{6,34},{8,64},{10,66},{12,96},{14,98},{16,128},... | collective-permute-start | bytes 20 | tf_op jit(solution)/shard_map/ppermute | solution.py:594
  9.6 0.8 copy.18
  10.6 4.1 %collective-permute-start = (s32[256]{0:T(256)S(1)}, s32[256]{0:T(256)S(1)}, u32[]{:S(2)}, u32[]{:S(2)}) collective-permute-start(s32[256]{0:T(256)S(1)} %reshape_squeeze.3.kept), channel_id=1, source_target_pairs={{0,0},{2,2},{4,32},{6,34},{8,64},{10,66},{12,96},{14,98},{16,128},... | collective-permute-start | bytes 3080 | tf_op jit(solution)/shard_map/ppermute | solution.py:593
  14.7 1.3 fusion.2
  16.0 0.8 reshape.202
  17.5 1.3 and_select_fusion.1
  18.8 1.3 copy.25
  20.1 6.5 %copy.19 = bf16[32,16,4096]{2,1,0:T(8,128)(2,1)} copy(bf16[32,16,4096]{2,0,1:T(8,128)(2,1)} %bitcast.38) | data formatting | bytes 8388608 | tf_op jit(solution)/shard_map/transpose | solution.py:608
  26.6 79.8 %spread.1 = (bf16[2,16,16,4096]{3,2,1,0:T(8,128)(2,1)}, bf16[2,8,32,4096]{3,2,1,0:T(8,128)(2,1)}, bf16[2,16,32,4096]{3,2,1,0:T(8,128)(2,1)}) custom-call(bf16[8,2,2,16,4096]{4,3,2,1,0:T(8,128)(2,1)} %bitcast.32, bf16[2,32,4096]{2,1,0:T(8,128)(2,1)S(1)} %bitcast.31), custom_call_target="tpu_custom_call" | custom-call | tf_op jit(solution)/shard_map/spread/pallas_call | solution.py:218
  107.5 2.5 collective-permute-start.1
  109.9 0.8 subtract_subtract_fusion.divisor
  110.8 18.6 %cross.1 = (f32[128,64,128]{2,1,0:T(8,128)}, bf16[128,64,128]{2,1,0:T(8,128)(2,1)}) custom-call(s32[520]{0:T(1024)S(1)} %pad_add_fusion.kept, bf16[2,256,4096]{2,1,0:T(8,128)(2,1)} %bitcast.40, bf16[2,256,4096]{2,1,0:T(8,128)(2,1)} %bitcast.42), custom_call_target="tpu_custom_call" | custom-call | tf_op jit(solution)/shard_map/cross/pallas_call | solution.py:276
  129.5 78.9 %amplitudes.1 = (bf16[2,128,64,128]{3,2,1,0:T(8,128)(2,1)}, bf16[16,64,128]{2,1,0:T(8,128)(2,1)S(1)}) custom-call(f32[128,64,128]{2,1,0:T(8,128)} %get-tuple-element.15.own, bf16[128,64,128]{2,1,0:T(8,128)(2,1)} %get-tuple-element.16.other, f32[16,64,128]{2,1,0:T(8,128)S(1)} %subtract_subtract_fusion.divisor), custom_call_target="tpu_custom_call" | custom-call | tf_op jit(solution)/shard_map/amplitudes/pallas_call | solution.py:431
  208.4 1.8 broadcast_in_dim.47
  210.3 14.7 %all-to-all-start = ((bf16[8,16,64,128]{3,2,1,0:T(8,128)(2,1)}), bf16[8,16,64,128]{3,2,1,0:T(8,128)(2,1)S(1)}, u32[]{:S(2)}, u32[]{:S(2)}) async-start(bf16[8,16,64,128]{3,2,1,0:T(8,128)(2,1)} %broadcast_in_dim.47), calls=%async_computation | async-start | bytes 4194304 | tf_op jit(solution)/shard_map/all_to_all | solution.py:618
  225.0 19.2 %toward_first.1 = bf16[8,2,32,4096]{3,2,1,0:T(8,128)(2,1)} custom-call(s32[520]{0:T(1024)S(1)} %pad_add_fusion.kept, bf16[2,256,4096]{2,1,0:T(8,128)(2,1)} %bitcast.41, bf16[2,128,64,128]{3,2,1,0:T(8,128)(2,1)} %get-tuple-element.18.amp), custom_call_target="tpu_custom_call" | custom-call | flops 4294967296 | bytes 25165824 | tf_op jit(solution)/shard_map/toward_first/pallas_call | solution.py:498
  244.2 7.7 %all-to-all-done = bf16[8,16,64,128]{3,2,1,0:T(8,128)(2,1)S(1)} async-done(((bf16[8,16,64,128]{3,2,1,0:T(8,128)(2,1)}), bf16[8,16,64,128]{3,2,1,0:T(8,128)(2,1)S(1)}, u32[]{:S(2)}, u32[]{:S(2)}) %all-to-all-start) | async-done | bytes 2097184 | tf_op jit(solution)/shard_map/all_to_all | solution.py:618
  251.9 1.3 copy-done
  253.3 9.2 %all-to-all-start.1 = ((bf16[16,32,4096]{2,1,0:T(8,128)(2,1)}), bf16[16,32,4096]{2,1,0:T(8,128)(2,1)}, u32[]{:S(2)}, u32[]{:S(2)}) async-start(bf16[16,32,4096]{2,1,0:T(8,128)(2,1)} %bitcast.39), calls=%async_computation.1 | async-start | bytes 8388608 | tf_op jit(solution)/shard_map/all_to_all | solution.py:623
  262.4 23.3 %toward_second.2.rest_0_ = bf16[512,4096]{1,0:T(8,128)(2,1)} custom-call(s32[256]{0:T(256)S(1)} %reshape_squeeze.3.kept, bf16[2,512,4096]{2,1,0:T(8,128)(2,1)} %bitcast.33, bf16[128,64,128]{2,1,0:T(8,128)(2,1)} %bitcast.35), custom_call_target="tpu_custom_call" | custom-call | flops 6442450944 | bytes 100663296 | tf_op jit(solution)/shard_map/toward_second/pallas_call | solution.py:560
  285.7 38.8 %all-to-all-done.1 = bf16[16,32,4096]{2,1,0:T(8,128)(2,1)} async-done(((bf16[16,32,4096]{2,1,0:T(8,128)(2,1)}), bf16[16,32,4096]{2,1,0:T(8,128)(2,1)}, u32[]{:S(2)}, u32[]{:S(2)}) %all-to-all-start.1) | async-done | bytes 4194336 | tf_op jit(solution)/shard_map/all_to_all | solution.py:623
  324.5 3.0 reduce_sum.12
  328.2 7.5 %all-to-all-start.2 = ((bf16[32,16,256]{2,0,1:T(8,128)(2,1)}), bf16[32,16,256]{2,0,1:T(8,128)(2,1)S(1)}, u32[]{:S(2)}, u32[]{:S(2)}) async-start(bf16[32,16,256]{2,0,1:T(8,128)(2,1)} %bitcast.30), calls=%async_computation.2 | async-start | bytes 524288 | tf_op jit(solution)/shard_map/all_to_all | solution.py:628
  335.8 13.9 %toward_second.3 = bf16[512,4096]{1,0:T(8,128)(2,1)} custom-call(s32[256]{0:T(256)S(1)} %reshape_squeeze.3.kept, bf16[2,512,4096]{2,1,0:T(8,128)(2,1)} %bitcast.34, bf16[128,64,128]{2,1,0:T(8,128)(2,1)} %bitcast.36, bf16[512,4096]{1,0:T(8,128)(2,1)} %toward_second.2.rest_0_), custom_call_target="tpu_custom_call", output_to_operand_aliasing={{}: (3, {})} | custom-call | flops 2147483648 | bytes 33554432 | tf_op jit(solution)/shard_map/toward_second/pallas_call | solution.py:560
  (23 shorter events, 3.3 us)
Async XLA Ops:
  0.6 109.3 %collective-permute-start.2 = (f32[1]{0:T(128)}, f32[1]{0:T(128)}, u32[]{:S(2)}, u32[]{:S(2)}) collective-permute-start(f32[1]{0:T(128)} %param.9), channel_id=1, source_target_pairs={{0,0},{2,2},{4,32},{6,34},{8,64},{10,66},{12,96},{14,98},{16,128},... | collective-permute-start | bytes 20 | tf_op jit(solution)/shard_map/ppermute | solution.py:594
  10.6 95.9 %collective-permute-start = (s32[256]{0:T(256)S(1)}, s32[256]{0:T(256)S(1)}, u32[]{:S(2)}, u32[]{:S(2)}) collective-permute-start(s32[256]{0:T(256)S(1)} %reshape_squeeze.3.kept), channel_id=1, source_target_pairs={{0,0},{2,2},{4,32},{6,34},{8,64},{10,66},{12,96},{14,98},{16,128},... | collective-permute-start | bytes 3080 | tf_op jit(solution)/shard_map/ppermute | solution.py:593
  107.5 3.3 collective-permute-start.1
  210.3 41.7 %all-to-all-start = ((bf16[8,16,64,128]{3,2,1,0:T(8,128)(2,1)}), bf16[8,16,64,128]{3,2,1,0:T(8,128)(2,1)S(1)}, u32[]{:S(2)}, u32[]{:S(2)}) async-start(bf16[8,16,64,128]{3,2,1,0:T(8,128)(2,1)} %broadcast_in_dim.47), calls=%async_computation | async-start | bytes 4194304 | tf_op jit(solution)/shard_map/all_to_all | solution.py:618
  251.9 1.3 copy-start
  253.3 71.2 %all-to-all-start.1 = ((bf16[16,32,4096]{2,1,0:T(8,128)(2,1)}), bf16[16,32,4096]{2,1,0:T(8,128)(2,1)}, u32[]{:S(2)}, u32[]{:S(2)}) async-start(bf16[16,32,4096]{2,1,0:T(8,128)(2,1)} %bitcast.39), calls=%async_computation.1 | async-start | bytes 8388608 | tf_op jit(solution)/shard_map/all_to_all | solution.py:623
  328.2 21.4 %all-to-all-start.2 = ((bf16[32,16,256]{2,0,1:T(8,128)(2,1)}), bf16[32,16,256]{2,0,1:T(8,128)(2,1)S(1)}, u32[]{:S(2)}, u32[]{:S(2)}) async-start(bf16[32,16,256]{2,0,1:T(8,128)(2,1)} %bitcast.30), calls=%async_computation.2 | async-start | bytes 524288 | tf_op jit(solution)/shard_map/all_to_all | solution.py:628

commit v3 on v2

--- a/solution.py
+++ b/solution.py
@@ -17,6 +17,7 @@
     (1, 0), (0, 1), (3, 0), (0, 3), (1, 1), (3, 3), (1, 3), (3, 1),
     (2, 0), (0, 2), (2, 1), (1, 2), (2, 3), (3, 2), (2, 2),
 )
+LINE = ((1, 0), (3, 0), (0, 1), (2, 0), (1, 1), (3, 1), (2, 1))
 VMEM_LIMIT = 52 * 1024 * 1024
 
 
@@ -243,65 +244,33 @@
     return ref[(*lead, slice(None), pl.ds(pl.multiple_of(block // 2 * LANES, LANES), LANES))]
 
 
-def cross_kernel(group, nb, kept, sec, first, own, other):
-    i, g = pl.program_id(0), pl.program_id(1)
+def load_tiles(sec_hbm, sec, sem):
+    return [
+        pltpu.make_async_copy(sec_hbm.at[:, :, pl.ds(t * LANES, LANES)], sec.at[:, t], sem.at[t])
+        for t in range(sec.shape[1])
+    ]
+
+
+def spread_masked(amp, straight):
     lane = lax.broadcasted_iota(jnp.int32, (BLK, LANES), 1)
-    for pairs in range(group // 2):
-        left = first[0, :, pairs * LANES:(pairs + 1) * LANES].T
-        for side, out in ((0, own), (1, other)):
-            for e in range(2):
-                entry = pairs * 2 + e
-                at = ((side * 2 + i) * nb + g * group + entry) * 2
-                b0, b1 = kept[at], kept[at + 1]
-                which = kept[4 * nb * 2] if side == 0 else 1 - kept[4 * nb * 2]
-                right = jnp.concatenate(
-                    [tile_of(sec, (which,), b0), tile_of(sec, (which,), b1)], axis=1
-                )
-                prod = lax.dot_general(
-                    left[e * BLK:(e + 1) * BLK], right, (((1,), (0,)), ((), ())),
-                    preferred_element_type=F32,
-                )
-                u0, u1 = prod[:, :LANES], prod[:, LANES:]
-                r0 = jnp.where(b0 % 2 == 0, u0, pltpu.roll(u0, BLK, 1))
-                r1 = jnp.where(b1 % 2 == 1, u1, pltpu.roll(u1, BLK, 1))
-                out[entry] = jnp.where(lane < BLK, r0, r1).astype(out.dtype)
-
-
-def cross(kept, sec, first, group=8):
-    _, rows, width = sec.shape
-    ni = first.shape[0]
-    nb = width // BLK
-    groups = nb // group
-    entries = ni * nb
-    return pl.pallas_call(
-        functools.partial(cross_kernel, group, nb),
-        out_shape=[
-            jax.ShapeDtypeStruct((entries, BLK, LANES), F32),
-            jax.ShapeDtypeStruct((entries, BLK, LANES), BF16),
-        ],
-        grid_spec=pltpu.PrefetchScalarGridSpec(
-            num_scalar_prefetch=1,
-            grid=(ni, groups),
-            in_specs=[
-                pl.BlockSpec((2, rows, width), lambda i, g, kept: (0, 0, 0)),
-                pl.BlockSpec((1, rows, group * BLK), lambda i, g, kept: (i, 0, g)),
-            ],
-            out_specs=[
-                pl.BlockSpec((group, BLK, LANES), lambda i, g, kept: (i * groups + g, 0, 0)),
-                pl.BlockSpec((group, BLK, LANES), lambda i, g, kept: (i * groups + g, 0, 0)),
-            ],
-        ),
-        compiler_params=pltpu.CompilerParams(vmem_limit_bytes=VMEM_LIMIT),
-        name="cross",
-    )(kept, sec, first)
+    zero = jnp.zeros_like(amp)
+    stay = jnp.where(straight, amp, zero)
+    move = pltpu.roll(jnp.where(straight, zero, amp), BLK, 1)
+    return jnp.where(lane < BLK, stay, move), jnp.where(lane < BLK, move, stay)
 
 
 def amplitude_kernel(
-    naux, nz, own, other, divisor, amp1, amp2,
-    twin, outgoing, got, shard, d_send, d_recv, r_send, r_recv, t_send, t_recv, loc, *sems
+    naux, nz, nb, tiles, sec_hbm, first_hbm, straight, divisor, amp1, amp2,
+    sec, first, own, other, twin, outgoing, got, shard,
+    d_send, d_recv, r_send, r_recv, t_send, t_recv, x_send, x_recv, s_load, loc, *sems
 ):
     a, z, c, p = place()
+    x, yh = a // 2, a % 2
     size = divisor.shape[0]
+    loads = [pltpu.make_async_copy(first_hbm, first, loc.at[2]), *load_tiles(sec_hbm, sec, s_load)]
+    for load in loads:
+        load.start()
+    far, half = nz // 2, size // 2
 
     def me(dz, dc):
         return device(a, (z + dz) % nz, (c + dc) % 2, p)
@@ -309,7 +278,10 @@
     sibling = me(0, 1)
     mirror = device(z, a, c, p)
     barrier = pltpu.get_barrier_semaphore()
-    peers = [sibling, me(1, 0), me(nz - 1, 0)]
+    line = [
+        device((x + dx) % NX * 2 + (yh + dy) % 2, z, c, p) for dx, dy in LINE
+    ]
+    peers = [sibling, me(1, 0), me(nz - 1, 0)] + line
     for peer in peers:
         pl.semaphore_signal(barrier, inc=1, device_id=peer, device_id_type=MESH)
 
@@ -322,56 +294,95 @@
     def _():
         pl.semaphore_wait(barrier, len(peers))
 
+    for load in loads:
+        load.wait()
+    lane = lax.broadcasted_iota(jnp.int32, (BLK, LANES), 1)
+
     def rows(t):
         return pl.ds(t * size, size)
 
-    far, half = nz // 2, size // 2
-    order = sorted(range(nz), key=lambda d: (-min(d, nz - d), d))
     sent = []
-    for dz in order:
-        part = rows((z + dz) % nz)
-        sent.append(push(other.at[part], twin.at[part], d_send.at[dz], d_recv.at[dz], sibling))
+
+    def compute(dz):
+        t = (z + dz) % nz
+        i, start = t * size // nb, t * size % nb
+
+        def two(k, _):
+            tile = pl.ds(pl.multiple_of((start // 2 + k) * LANES, LANES), LANES)
+            left = first[i, :, tile].T
+            for side, out in ((0, own), (1, other)):
+                which = c if side == 0 else 1 - c
+                for e in range(2):
+                    at = (side * 2 + i) * nb + start + k * 2 + e
+                    right = jnp.concatenate(
+                        [sec[which, tiles[at * 2]], sec[which, tiles[at * 2 + 1]]], axis=1
+                    )
+                    prod = lax.dot_general(
+                        left[e * BLK:(e + 1) * BLK], right, (((1,), (0,)), ((), ())),
+                        preferred_element_type=F32,
+                    )
+                    u0, u1 = prod[:, :LANES], prod[:, LANES:]
+                    stay = jnp.where(lane < BLK, u0, u1)
+                    move = pltpu.roll(jnp.where(lane < BLK, u1, u0), BLK, 1)
+                    chosen = jnp.where(straight[pl.ds(at, 1), :] > 0.5, stay, move)
+                    out[t * size + k * 2 + e] = chosen.astype(out.dtype)
+            return 0
+
+        lax.fori_loop(0, size // 2, two, 0)
+        sent.append(
+            push(other.at[rows(t)], twin.at[rows(t)], d_send.at[dz], d_recv.at[dz], sibling)
+        )
+
     ways = ((1, 0, me(1, 0)), (-1, 1, me(nz - 1, 0)))
-    for step in range(far):
-        for way, w, to in ways:
-            dz = way * (far - step) % nz
-            t = (z + dz) % nz
-            if step or w == 0:
-                landed(twin.at[rows(t)], d_send.at[dz], d_recv.at[dz], sibling)
-            first_row = w * half if step == 0 else 0
-            count = half if step == 0 else size
-            if step:
-                before = pl.ds(w * half, half) if step == 1 else pl.ds(0, size)
-                come = got.at[w, step - 1, before]
-                landed(come, r_send.at[w, step - 1], r_recv.at[w, step - 1], to)
-
-            def add(k, _):
-                n = t * size + k
-                total = own[n] + twin[n].astype(F32)
-                outgoing[w, step, k] = total.astype(BF16)
-                return 0
-
-            def add_got(k, _):
-                n = t * size + k
-                total = own[n] + twin[n].astype(F32) + got[w, step - 1, k].astype(F32)
-                outgoing[w, step, k] = total.astype(BF16)
-                return 0
-
-            if step == 0:
-                lax.fori_loop(first_row, first_row + count, add, 0)
-            elif step == 1:
-                lax.fori_loop(w * half, w * half + half, add_got, 0)
-                lax.fori_loop((1 - w) * half, (1 - w) * half + half, add, 0)
+
+    def reduce_step(step, way, w, to):
+        dz = way * (far - step) % nz
+        t = (z + dz) % nz
+        if step or w == 0:
+            landed(twin.at[rows(t)], d_send.at[dz], d_recv.at[dz], sibling)
+
+        def add(k, _):
+            n = t * size + k
+            total = own[n] + twin[n].astype(F32)
+            outgoing[w, step, k] = total.astype(BF16)
+            return 0
+
+        def add_got(k, _):
+            n = t * size + k
+            total = own[n] + twin[n].astype(F32) + got[w, step - 1, k].astype(F32)
+            outgoing[w, step, k] = total.astype(BF16)
+            return 0
+
+        for h in (1 - w, w):
+            if step == 0 and h != w:
+                continue
+            span = pl.ds(h * half, half)
+            if step > 1 or (step == 1 and h == w):
+                landed(got.at[w, step - 1, span], r_send.at[w, step - 1, h],
+                       r_recv.at[w, step - 1, h], to)
+                lax.fori_loop(h * half, h * half + half, add_got, 0, unroll=4)
             else:
-                lax.fori_loop(0, size, add_got, 0)
-            span = pl.ds(first_row, count)
+                lax.fori_loop(h * half, h * half + half, add, 0, unroll=4)
             sent.append(
                 push(outgoing.at[w, step, span], got.at[w, step, span],
-                     r_send.at[w, step], r_recv.at[w, step], to)
+                     r_send.at[w, step, h], r_recv.at[w, step, h], to)
             )
+
+    compute(far)
+    compute(far - 1)
+    reduce_step(0, *ways[0])
+    reduce_step(0, *ways[1])
+    for step in range(1, far):
+        compute(nz - far + step)
+        reduce_step(step, *ways[0])
+        compute(far - 1 - step)
+        reduce_step(step, *ways[1])
+
     landed(twin.at[rows(z)], d_send.at[0], d_recv.at[0], sibling)
     for way, w, to in ways:
-        landed(got.at[w, far - 1], r_send.at[w, far - 1], r_recv.at[w, far - 1], to)
+        for h in range(2):
+            landed(got.at[w, far - 1, pl.ds(h * half, half)], r_send.at[w, far - 1, h],
+                   r_recv.at[w, far - 1, h], to)
 
     def reduce(k, _):
         n = z * size + k
@@ -380,80 +391,86 @@
         shard[k] = (total / divisor[k]).astype(BF16)
         return 0
 
-    lax.fori_loop(0, size, reduce, 0)
+    lax.fori_loop(0, size, reduce, 0, unroll=2)
 
     ring = Ring(
         lambda zz, cc: amp1.at[cc, pl.ds(zz * size, size)],
         lambda zz, cc, h: amp1.at[cc, pl.ds(zz * size + h * half, half)],
         z, nz, c, lambda dz, dc: me((dz + nz) % nz, dc), sems,
     )
-
     @pl.when(a != z)
     def _():
-        push(shard, amp2, t_send.at[0], t_recv.at[0], mirror)
+        push(shard, amp2.at[z], t_send.at[0], t_recv.at[0], mirror)
 
     @pl.when(a == z)
     def _():
-        pltpu.make_async_copy(shard, amp2, loc.at[0]).start()
+        pltpu.make_async_copy(shard, amp2.at[z], loc.at[0]).start()
 
     ring.start(shard, None)
     here = pltpu.make_async_copy(shard, amp1.at[c, rows(z)], loc.at[1])
     here.start()
-
-    for step in range(nz // 2):
+    ring.step(0)
+
+    @pl.when(a != z)
+    def _():
+        landed(amp2.at[a], t_send.at[0], t_recv.at[0], mirror)
+        pltpu.make_async_remote_copy(
+            src_ref=shard, dst_ref=amp2.at[z], send_sem=t_send.at[0], recv_sem=t_recv.at[0],
+            device_id=mirror, device_id_type=MESH,
+        ).wait_send()
+
+    @pl.when(a == z)
+    def _():
+        pltpu.make_async_copy(shard, amp2.at[z], loc.at[0]).wait()
+
+    for n, peer in enumerate(line):
+        sent.append(push(amp2.at[a], amp2.at[a], x_send.at[n], x_recv.at[n], peer))
+    for step in range(1, far):
         ring.step(step)
     ring.finish()
-
-    @pl.when(a != z)
-    def _():
-        landed(amp2, t_send.at[0], t_recv.at[0], mirror)
-
-    @pl.when(a == z)
-    def _():
-        pltpu.make_async_copy(shard, amp2, loc.at[0]).wait()
-
+    for n, (dx, dy) in enumerate(LINE):
+        fa = (x - dx + NX) % NX * 2 + (yh + dy) % 2
+        landed(amp2.at[fa], x_send.at[n], x_recv.at[n], device(fa, z, c, p))
     here.wait()
     for copy in sent:
         copy.wait_send()
 
-    @pl.when(a != z)
-    def _():
-        pltpu.make_async_remote_copy(
-            src_ref=shard, dst_ref=amp2, send_sem=t_send.at[0], recv_sem=t_recv.at[0],
-            device_id=mirror, device_id_type=MESH,
-        ).wait_send()
-
-
-def amplitudes(own, other, divisor, naux, nz):
-    entries, rows, lanes = own.shape
+
+def amplitudes(tiles, sec, first, straight, divisor, naux, nz):
+    ni, _, width = first.shape
+    nb = width // BLK
+    entries = ni * nb
     size = divisor.shape[0]
+    block = (BLK, LANES)
     dma = pltpu.SemaphoreType.DMA
+    vmem = pl.BlockSpec(memory_space=pltpu.VMEM)
+    hbm = pl.BlockSpec(memory_space=pl.ANY)
     return pl.pallas_call(
-        functools.partial(amplitude_kernel, naux, nz),
+        functools.partial(amplitude_kernel, naux, nz, nb),
         out_shape=[
-            jax.ShapeDtypeStruct((2, entries, rows, lanes), BF16),
-            jax.ShapeDtypeStruct((size, rows, lanes), BF16),
+            jax.ShapeDtypeStruct((2, entries, *block), BF16),
+            jax.ShapeDtypeStruct((naux, size, *block), BF16),
         ],
-        in_specs=[
-            pl.BlockSpec(memory_space=pltpu.VMEM),
-            pl.BlockSpec(memory_space=pl.ANY),
-            pl.BlockSpec(memory_space=pltpu.VMEM),
-        ],
-        out_specs=[pl.BlockSpec(memory_space=pl.ANY)] * 2,
+        in_specs=[pl.BlockSpec(memory_space=pltpu.SMEM), hbm, hbm, vmem, vmem],
+        out_specs=[hbm, hbm],
         scratch_shapes=[
-            pltpu.VMEM((entries, rows, lanes), BF16),
-            pltpu.VMEM((2, nz // 2, size, rows, lanes), BF16),
-            pltpu.VMEM((2, nz // 2, size, rows, lanes), BF16),
-            pltpu.VMEM((size, rows, lanes), BF16),
-            dma((nz,)), dma((nz,)), dma((2, nz // 2)), dma((2, nz // 2)), dma((1,)), dma((1,)),
-            dma((2,)),
+            pltpu.VMEM((2, width // LANES, sec.shape[1], LANES), BF16),
+            pltpu.VMEM(first.shape, BF16),
+            pltpu.VMEM((entries, *block), F32),
+            pltpu.VMEM((entries, *block), BF16),
+            pltpu.VMEM((entries, *block), BF16),
+            pltpu.VMEM((2, nz // 2, size, *block), BF16),
+            pltpu.VMEM((2, nz // 2, size, *block), BF16),
+            pltpu.VMEM((size, *block), BF16),
+            dma((nz,)), dma((nz,)), dma((2, nz // 2, 2)), dma((2, nz // 2, 2)), dma((1,)), dma((1,)),
+            dma((naux - 1,)), dma((naux - 1,)), dma((width // LANES,)), dma((3,)),
             *ring_sems(nz),
         ],
         compiler_params=pltpu.CompilerParams(
             collective_id=2, has_side_effects=True, vmem_limit_bytes=VMEM_LIMIT
         ),
         name="amplitudes",
-    )(own, other, divisor)
+    )(tiles, sec, first, straight, divisor)
 
 
 def spread_halves(amp, b0, b1):
@@ -465,60 +482,226 @@
     return t0, t1
 
 
-def toward_first_kernel(group, nb, kept, sec, amp, out):
-    i, g = pl.program_id(0), pl.program_id(1)
-    naux, _, frows, _ = out.shape
-    for pairs in range(group // 2):
-        halves = []
-        for e in range(2):
-            entry = pairs * 2 + e
-            tiles, weights = [], []
-            for core in range(2):
-                side = jnp.where(kept[4 * nb * 2] == core, 0, 1)
-                at = ((side * 2 + i) * nb + g * group + entry) * 2
-                b0, b1 = kept[at], kept[at + 1]
-                tiles += [tile_of(sec, (core,), b0), tile_of(sec, (core,), b1)]
-                weights += spread_halves(amp[core, entry].astype(F32), b0, b1)
-            halves.append(
-                lax.dot_general(
-                    jnp.concatenate(tiles, axis=1),
-                    jnp.concatenate(weights, axis=1).astype(BF16),
-                    (((1,), (1,)), ((), ())),
-                    preferred_element_type=F32,
+class Sum:
+    def __init__(self, me, up, dn, s0, r0, s1, r1):
+        self.me, self.up, self.dn = me, up, dn
+        self.s0, self.r0, self.s1, self.r1 = s0, r0, s1, r1
+
+    def first(self, part, into):
+        far = (self.me + 2) % 4
+        return [
+            push(part(far, w), into(w), self.s0.at[w], self.r0.at[w], to)
+            for w, to in ((0, self.up), (1, self.dn))
+        ]
+
+    def first_landed(self, into):
+        for w, to in ((0, self.dn), (1, self.up)):
+            landed(into(w), self.s0.at[w], self.r0.at[w], to)
+
+    def second(self, source, into):
+        return [
+            push(source(w), into(w), self.s1.at[w], self.r1.at[w], to)
+            for w, to in ((0, self.up), (1, self.dn))
+        ]
+
+    def second_landed(self, into):
+        for w, to in ((0, self.dn), (1, self.up)):
+            landed(into(w), self.s1.at[w], self.r1.at[w], to)
+
+
+def first_density_kernel(
+    naux, nz, nb, tiles, sec_hbm, amp_hbm, straight, out,
+    sec, amp, part, got_a, give_b, got_b, total, give_c, got_c, give_d, got_d, done,
+    p1s, p1r, p2s, p2r, z_send, z_recv, s_load, loc
+):
+    a, z, c, p = place()
+    loads = [pltpu.make_async_copy(amp_hbm, amp, loc.at[0]), *load_tiles(sec_hbm, sec, s_load)]
+    for load in loads:
+        load.start()
+    x, y = a // 2, a % 2 * 2 + p
+    frows, width = part.shape[3], part.shape[4]
+    group = width // BLK
+    chunk_half = width // 2
+
+    def me(dz, dc):
+        return device(a, (z + dz) % nz, (c + dc) % 2, p)
+
+    def at_y(ty):
+        return device(x * 2 + ty // 2, z, c, ty % 2)
+
+    column = [(dz, dc) for dz in range(nz) for dc in range(2) if (dz, dc) != (0, 0)]
+    right, left = device((a + 2) % naux, z, c, p), device((a + naux - 2) % naux, z, c, p)
+    above, below = at_y((y + 1) % 4), at_y((y + 3) % 4)
+    greet([right, left, above, below] + [me(dz, dc) for dz, dc in column])
+    for load in loads:
+        load.wait()
+    sent = []
+
+    def compute(k):
+        chunk = (z + 1 + k) % nz
+
+        def orbital(i, _):
+            for m in range(group // 2):
+                halves = []
+                for e in range(2):
+                    entry = chunk * group + m * 2 + e
+                    rights, weights = [], []
+                    for side in range(2):
+                        core = c if side == 0 else 1 - c
+                        at = (side * 2 + i) * nb + entry
+                        rights += [sec[core, tiles[at * 2]], sec[core, tiles[at * 2 + 1]]]
+                        weights += spread_masked(
+                            amp[core, i * nb + entry].astype(F32), straight[pl.ds(at, 1), :] > 0.5
+                        )
+                    halves.append(
+                        lax.dot_general(
+                            jnp.concatenate(rights, axis=1),
+                            jnp.concatenate(weights, axis=1).astype(BF16),
+                            (((1,), (1,)), ((), ())),
+                            preferred_element_type=F32,
+                        )
+                    )
+                both = jnp.concatenate(halves, axis=1).astype(BF16)
+                both = both.reshape(4, 2, frows, LANES)
+                cols = slice(m * LANES, (m + 1) * LANES)
+                for xx in range(4):
+                    for yy in range(2):
+                        u, v = (xx, yy * 2 + i) if k % 2 == 0 else (yy * 2 + i, xx)
+                        part[k, u, v, :, cols] = both[xx, yy]
+            return 0
+
+        lax.fori_loop(0, 2, orbital, 0)
+
+    def rings(k):
+        over_x = (x, right, left)
+        over_y = (y, above, below)
+        one, two = (over_x, over_y) if k % 2 == 0 else (over_y, over_x)
+        return (
+            Sum(*one, p1s.at[k, 0], p1r.at[k, 0], p1s.at[k, 1], p1r.at[k, 1]),
+            Sum(*two, p2s.at[k, 0], p2r.at[k, 0], p2s.at[k, 1], p2r.at[k, 1]),
+        )
+
+    def stage_b(k):
+        one, _ = rings(k)
+        sent.extend(
+            one.first(
+                lambda far, w: part.at[k, far, pl.ds(2 * w, 2)], lambda w: got_a.at[k, w]
+            )
+        )
+
+    def stage_c(k):
+        one, _ = rings(k)
+        one.first_landed(lambda w: got_a.at[k, w])
+        for w, step in ((0, 1), (1, 3)):
+            u = (one.me + step) % 4
+            for v in range(4):
+                if v // 2 == w:
+                    both = part[k, u, v].astype(F32) + got_a[k, w, v % 2].astype(F32)
+                    give_b[k, w, v] = both.astype(BF16)
+                else:
+                    give_b[k, w, v] = part[k, u, v]
+        sent.extend(one.second(lambda w: give_b.at[k, w], lambda w: got_b.at[k, w]))
+
+    def stage_d(k):
+        one, two = rings(k)
+        one.second_landed(lambda w: got_b.at[k, w])
+        for v in range(4):
+            total[k, v] = (
+                part[k, one.me, v].astype(F32)
+                + got_b[k, 0, v].astype(F32) + got_b[k, 1, v].astype(F32)
+            )
+        far = (two.me + 2) % 4
+        for w in range(2):
+            give_c[k, w] = total[k, far, :, w * chunk_half:(w + 1) * chunk_half].astype(BF16)
+        sent.extend(two.first(lambda far, w: give_c.at[k, w], lambda w: got_c.at[k, w]))
+
+    def stage_e(k):
+        _, two = rings(k)
+        two.first_landed(lambda w: got_c.at[k, w])
+        for w, step in ((0, 1), (1, 3)):
+            v = (two.me + step) % 4
+            for h in range(2):
+                cols = slice(h * chunk_half, (h + 1) * chunk_half)
+                mine = total[k, v, :, cols]
+                if h == w:
+                    mine = mine + got_c[k, w].astype(F32)
+                give_d[k, w, :, cols] = mine.astype(BF16)
+        sent.extend(two.second(lambda w: give_d.at[k, w], lambda w: got_d.at[k, w]))
+
+    def stage_f(k):
+        _, two = rings(k)
+        two.second_landed(lambda w: got_d.at[k, w])
+        final = total[k, two.me] + got_d[k, 0].astype(F32) + got_d[k, 1].astype(F32)
+        done[k] = final.astype(BF16)
+        dz = (k + 1) % nz
+        for dc in range(2):
+            cc = (c + dc) % 2
+            source = done.at[k, :, pl.ds(pl.multiple_of(cc * chunk_half, chunk_half), chunk_half)]
+            if (dz, dc) == (0, 0):
+                pltpu.make_async_copy(source, out.at[z * 2 + c], loc.at[1]).start()
+            else:
+                n = dz * 2 + dc
+                sent.append(
+                    push(source, out.at[z * 2 + c], z_send.at[n], z_recv.at[n], me(dz, dc))
                 )
-            )
-        both = jnp.concatenate(halves, axis=1).astype(BF16)
-        out[:, 0, :, pairs * LANES:(pairs + 1) * LANES] = both.reshape(naux, frows, LANES)
-
-
-def toward_first(kept, sec, amp, ni, naux, group=8):
+
+    stages = (stage_b, stage_c, stage_d, stage_e, stage_f)
+    for k in range(nz + len(stages) - 1):
+        if k < nz:
+            compute(k)
+        for lag, stage in enumerate(stages):
+            if 0 <= k - lag < nz:
+                stage(k - lag)
+
+    for dz, dc in column:
+        fz, fc = (z - dz + nz) % nz, (c + dc) % 2
+        n = dz * 2 + dc
+        landed(out.at[fz * 2 + fc], z_send.at[n], z_recv.at[n], device(a, fz, fc, p))
+    pltpu.make_async_copy(
+        done.at[nz - 1, :, pl.ds(pl.multiple_of(c * chunk_half, chunk_half), chunk_half)],
+        out.at[z * 2 + c], loc.at[1],
+    ).wait()
+    for copy in sent:
+        copy.wait_send()
+
+
+def first_density_of(tiles, sec, amp, straight, naux, nz):
     _, rows, width = sec.shape
     nb = width // BLK
-    groups = nb // group
+    frows, chunk = rows // naux, width // nz
+    dma = pltpu.SemaphoreType.DMA
+    hbm = pl.BlockSpec(memory_space=pl.ANY)
     return pl.pallas_call(
-        functools.partial(toward_first_kernel, group, nb),
-        out_shape=jax.ShapeDtypeStruct((naux, ni, rows // naux, width), BF16),
-        grid_spec=pltpu.PrefetchScalarGridSpec(
-            num_scalar_prefetch=1,
-            grid=(ni, groups),
-            in_specs=[
-                pl.BlockSpec((2, rows, width), lambda i, g, kept: (0, 0, 0)),
-                pl.BlockSpec((2, group, BLK, LANES), lambda i, g, kept: (0, i * groups + g, 0, 0)),
-            ],
-            out_specs=pl.BlockSpec(
-                (naux, 1, rows // naux, group * BLK), lambda i, g, kept: (0, i, 0, g)
-            ),
+        functools.partial(first_density_kernel, naux, nz, nb),
+        out_shape=jax.ShapeDtypeStruct((nz * 2, frows, chunk // 2), BF16),
+        in_specs=[
+            pl.BlockSpec(memory_space=pltpu.SMEM), hbm, hbm, pl.BlockSpec(memory_space=pltpu.VMEM)
+        ],
+        out_specs=hbm,
+        scratch_shapes=[
+            pltpu.VMEM((2, width // LANES, rows, LANES), BF16),
+            pltpu.VMEM(amp.shape, BF16),
+            pltpu.VMEM((nz, 4, 4, frows, chunk), BF16),
+            pltpu.VMEM((nz, 2, 2, frows, chunk), BF16),
+            pltpu.VMEM((nz, 2, 4, frows, chunk), BF16),
+            pltpu.VMEM((nz, 2, 4, frows, chunk), BF16),
+            pltpu.VMEM((nz, 4, frows, chunk), F32),
+            pltpu.VMEM((nz, 2, frows, chunk // 2), BF16),
+            pltpu.VMEM((nz, 2, frows, chunk // 2), BF16),
+            pltpu.VMEM((nz, 2, frows, chunk), BF16),
+            pltpu.VMEM((nz, 2, frows, chunk), BF16),
+            pltpu.VMEM((nz, frows, chunk), BF16),
+            dma((nz, 2, 2)), dma((nz, 2, 2)), dma((nz, 2, 2)), dma((nz, 2, 2)),
+            dma((nz * 2,)), dma((nz * 2,)), dma((width // LANES,)), dma((2,)),
+        ],
+        compiler_params=pltpu.CompilerParams(
+            collective_id=3, has_side_effects=True, vmem_limit_bytes=VMEM_LIMIT
         ),
-        compiler_params=pltpu.CompilerParams(vmem_limit_bytes=VMEM_LIMIT),
-        cost_estimate=pl.CostEstimate(
-            flops=ni * nb * BLK * rows * 4 * LANES * 4, bytes_accessed=24 << 20, transcendentals=0
-        ),
-        name="toward_first",
-    )(kept, sec, amp)
-
-
-def toward_second_kernel(group, nb, kept, first, amp, *rest):
-    out, total = rest[-2:]
+        name="first_density",
+    )(tiles, sec, amp, straight)
+
+
+def toward_second_kernel(group, nb, kept, first, amp, out, total):
     i, g = pl.program_id(0), pl.program_id(1)
 
     @pl.when((i == 0) & (g == 0))
@@ -545,36 +728,26 @@
         out[...] = total[...].astype(BF16)
 
 
-def toward_second(kept, first, amp, height, place_of, before, group=8):
+def toward_second(kept, first, amp, group=8):
     ni, rows, width = first.shape
     nb = width // BLK
     groups = nb // group
-    in_specs = [
-        pl.BlockSpec((1, height, group * BLK), lambda i, g, kept: (i, place_of, g)),
-        pl.BlockSpec((group, BLK, LANES), lambda i, g, kept: (i * groups + g, 0, 0)),
-    ]
-    operands = [kept, first, amp]
-    if before is not None:
-        in_specs.append(pl.BlockSpec(memory_space=pl.ANY))
-        operands.append(before)
     return pl.pallas_call(
         functools.partial(toward_second_kernel, group, nb),
         out_shape=jax.ShapeDtypeStruct((rows, width), BF16),
         grid_spec=pltpu.PrefetchScalarGridSpec(
             num_scalar_prefetch=1,
             grid=(ni, groups),
-            in_specs=in_specs,
-            out_specs=pl.BlockSpec((height, width), lambda i, g, kept: (place_of, 0)),
-            scratch_shapes=[pltpu.VMEM((height, width), F32)],
+            in_specs=[
+                pl.BlockSpec((1, rows, group * BLK), lambda i, g, kept: (i, 0, g)),
+                pl.BlockSpec((group, BLK, LANES), lambda i, g, kept: (i * groups + g, 0, 0)),
+            ],
+            out_specs=pl.BlockSpec((rows, width), lambda i, g, kept: (0, 0)),
+            scratch_shapes=[pltpu.VMEM((rows, width), F32)],
         ),
-        input_output_aliases={} if before is None else {3: 0},
         compiler_params=pltpu.CompilerParams(vmem_limit_bytes=VMEM_LIMIT),
-        cost_estimate=pl.CostEstimate(
-            flops=ni * nb * BLK * height * 4 * LANES * 4,
-            bytes_accessed=height << 18, transcendentals=0
-        ),
         name="toward_second",
-    )(*operands)
+    )(kept, first, amp)
 
 
 def shards(first_factors, second_factors, first_energy, second_energy, virtual_energy, kept_blocks):
@@ -594,7 +767,10 @@
     energy_mine = lax.ppermute(second_energy, ("aux", "occ"), order)
     swap = [(o, o // 2 * 2 + 1 - o % 2) for o in range(2 * nz)]
     kept_twin = lax.ppermute(kept_mine, "occ", swap)
-    kept = jnp.concatenate([kept_mine, kept_twin, jnp.full((8,), c, jnp.int32)])
+    kept = jnp.concatenate([kept_mine, kept_twin])
+    tiles = kept // 2
+    in_place = jnp.stack([kept[0::2] % 2 == 0, kept[1::2] % 2 == 1], axis=1)
+    straight = jnp.repeat(in_place.astype(F32), BLK, axis=1)
 
     size = entries // nz
     energy_blocks = virtual_energy.reshape(nb, BLK)
@@ -612,21 +788,10 @@
     firstz = firstz.reshape(ni, naux * frows, width)
     firsta = firsta.reshape(ni, nz * 2 * frows, width)
 
-    own, other = cross(kept, sec, firstz)
-    amp1, amp2 = amplitudes(own, other, divisor, naux, nz)
-    amp2 = jnp.broadcast_to(amp2[None], (naux, *amp2.shape))
-    amp2 = lax.all_to_all(amp2, "aux", split_axis=0, concat_axis=0, tiled=True)
+    amp1, amp2 = amplitudes(tiles, sec, firstz, straight, divisor, naux, nz)
+    first_density = first_density_of(tiles, sec, amp1, straight, naux, nz)
     amp2 = amp2.reshape(entries, BLK, LANES)
-
-    part = toward_first(kept, sec, amp1, ni, naux).reshape(naux * ni, frows, width)
-    amp2, part = lax.optimization_barrier((amp2, part))
-    terms = lax.all_to_all(part, ("aux", "pair"), split_axis=0, concat_axis=0, tiled=True)
-    most = nz * frows * 3 // 2
-    second_density = toward_second(kept_here, firsta, amp2, most, 0, None)
-    terms, second_density = lax.optimization_barrier((terms, second_density))
-    done = jnp.sum(terms.astype(F32), axis=0).astype(BF16)
-    first_density = lax.all_to_all(done, "occ", split_axis=1, concat_axis=0, tiled=True)
-    second_density = toward_second(kept_here, firsta, amp2, most // 3, 3, second_density)
+    second_density = toward_second(kept_here, firsta, amp2)
     return (
         first_density.reshape(nz * 2 * frows, 1, width // (nz * 2)),
         second_density.reshape(nz * 2 * frows, 1, width),

time: 352 us -> 295 us (0.84)
  waiting for transfers between devices: 46.5 us -> 0.81 us
  starting transfers between devices: 47 us -> 15.6 us
  Pallas kernels: 234 us -> 258 us
    all_to_all x3 -> x0, waiting for transfers between devices: 46.5 us -> none  [the longest x1 38.8 us: shards(): lax.all_to_all(part, ('aux', 'pair'), split_axis=0, concat_axis=0, tiled=...]
    pallas_call x3 -> x2, Pallas kernels: 117 us -> 149 us  [the longest x1 94.6 us: amplitudes(): pl.pallas_call(functools.partial(amplitude_kernel, naux, nz, nb), out_sha...]
    all_to_all x3 -> x0, starting transfers between devices: 31.5 us -> none  [the longest x1 14.7 us: shards(): amp2 = lax.all_to_all(amp2, 'aux', split_axis=0, concat_axis=0, tiled=True)]
    pallas_call x2 -> x1, Pallas kernels: 37.2 us -> 29.8 us  [toward_second(): pl.pallas_call(functools.partial(toward_second_kernel, group, nb), out_sh...]
  transfers between devices with their start and end apart: 6 -> 3, of which waited for: 2 -> 1; matrix products, arithmetic and copies ran while one was open for 4% -> 5% of each run, Pallas kernels for 39% -> 27%
where the time goes in v3:
time: 295 us; the launch traced here: 292 us
  Pallas kernels  258 us (87%)
  starting transfers between devices  15.6 us (5%)
  local copies, waits for them, and re-layouts  13.6 us (5%)
    pallas_call x1, Pallas kernels, amplitudes(): pl.pallas_call(functools.partial(amplitude_kernel, naux, nz, nb), out_sha...  94.6 us
    pallas_call x1, Pallas kernels, spread(): pl.pallas_call(functools.partial(spread_kernel, naux, nz), out_shape=[jax...  79.8 us
    pallas_call x1, Pallas kernels, first_density_of(): pl.pallas_call(functools.partial(first_density_kernel, naux, nz, nb), out...  54.3 us
    pallas_call x1, Pallas kernels, toward_second(): pl.pallas_call(functools.partial(toward_second_kernel, group, nb), out_sh...  29.8 us
    ppermute x1, starting transfers between devices, shards(): energy_mine = lax.ppermute(second_energy, ('aux', 'occ'), order)  8.99 us
    transpose x1, local copies, waits for them, and re-layouts, shards(): jnp.transpose(second_factors, (1, 0, 2)).reshape(naux, 2, 2, rows, width)  6.5 us
  transfers between devices with their start and end apart: 3, of which 1 were waited for; matrix products, arithmetic and copies ran while one was open for 5% of the time, Pallas kernels for 27%

profile of v3, /device:TPU:29, one launch (start us, length us, event | category | flops | bytes accessed | tf_op | source)
XLA Modules:
  0.0 291.6 jit_solution(8271457367428933765)
XLA Ops:
  0.6 9.0 %collective-permute-start.2 = (f32[1]{0:T(128)}, f32[1]{0:T(128)}, u32[]{:S(2)}, u32[]{:S(2)}) collective-permute-start(f32[1]{0:T(128)} %param.9), channel_id=1, source_target_pairs={{0,0},{2,2},{4,32},{6,34},{8,64},{10,66},{12,96},{14,98},{16,128},... | collective-permute-start | bytes 20 | tf_op jit(solution)/shard_map/ppermute | solution.py:767
  9.6 0.8 copy.10
  10.4 0.1 reshape_squeeze.3.kept
  10.6 4.1 %collective-permute-start = (s32[256]{0:T(256)S(1)}, s32[256]{0:T(256)S(1)}, u32[]{:S(2)}, u32[]{:S(2)}) collective-permute-start(s32[256]{0:T(256)S(1)} %reshape_squeeze.3.kept), channel_id=1, source_target_pairs={{0,0},{2,2},{4,32},{6,34},{8,64},{10,66},{12,96},{14,98},{16,128},... | collective-permute-start | bytes 3080 | tf_op jit(solution)/shard_map/ppermute | solution.py:766
  14.7 1.3 fusion.8
  16.0 0.8 reshape.198
  16.8 0.6 gather_fusion
  17.5 1.3 and_select_fusion.1
  18.8 1.3 copy.16
  20.1 6.5 %copy.11 = bf16[32,16,4096]{2,1,0:T(8,128)(2,1)} copy(bf16[32,16,4096]{2,0,1:T(8,128)(2,1)} %bitcast.32) | data formatting | bytes 8388608 | tf_op jit(solution)/shard_map/transpose | solution.py:784
  26.6 79.8 %spread.1 = (bf16[2,16,16,4096]{3,2,1,0:T(8,128)(2,1)}, bf16[2,8,32,4096]{3,2,1,0:T(8,128)(2,1)}, bf16[2,16,32,4096]{3,2,1,0:T(8,128)(2,1)}) custom-call(bf16[8,2,2,16,4096]{4,3,2,1,0:T(8,128)(2,1)} %bitcast.29, bf16[2,32,4096]{2,1,0:T(8,128)(2,1)S(1)} %bitcast.25), custom_call_target="tpu_custom_call" | custom-call | tf_op jit(solution)/shard_map/spread/pallas_call | solution.py:219
  106.5 0.1 broadcast_in_dim.36
  106.6 0.6 gather_fusion.1
  107.4 0.1 broadcast_in_dim.38
  107.5 0.8 subtract_subtract_fusion.divisor
  108.3 2.5 collective-permute-start.1
  110.8 0.8 collective-permute-done.1
  111.6 0.2 slice.7
  111.8 0.2 slice.6
  112.1 0.1 copy.13.straight
  112.2 94.6 %amplitudes.1 = (bf16[2,128,64,128]{3,2,1,0:T(8,128)(2,1)}, bf16[8,16,64,128]{3,2,1,0:T(8,128)(2,1)}) custom-call(s32[512]{0:T(512)S(1)} %add_select_fusion.tiles, bf16[2,256,4096]{2,1,0:T(8,128)(2,1)} %bitcast.27, bf16[2,256,4096]{2,1,0:T(8,128)(2,1)} %bitcast.31, f32[256,128]{1,0:T(8,128)S(1)} %copy.13.straight, ...), custom_call_target="tpu_custom_call" | custom-call | tf_op jit(solution)/shard_map/amplitudes/pallas_call | solution.py:448
  206.8 54.3 %first_density.1 = bf16[16,32,256]{2,1,0:T(8,128)(2,1)S(1)} custom-call(s32[512]{0:T(512)S(1)} %add_select_fusion.tiles, bf16[2,256,4096]{2,1,0:T(8,128)(2,1)} %bitcast.28, bf16[2,128,64,128]{3,2,1,0:T(8,128)(2,1)} %get-tuple-element.9.amp_hbm, f32[256,128]{1,0:T(8,128)S(1)} %copy.13.straight), custom_call_target="tpu_custom_call" | custom-call | tf_op jit(solution)/shard_map/first_density/pallas_call | solution.py:674
  261.2 29.8 %toward_second.1 = bf16[512,4096]{1,0:T(8,128)(2,1)} custom-call(s32[256]{0:T(256)S(1)} %reshape_squeeze.3.kept, bf16[2,512,4096]{2,1,0:T(8,128)(2,1)} %bitcast.30, bf16[128,64,128]{2,1,0:T(8,128)(2,1)} %bitcast.34), custom_call_target="tpu_custom_call" | custom-call | tf_op jit(solution)/shard_map/toward_second/pallas_call | solution.py:735
  290.9 0.7 copy.20
  (21 shorter events, 0.5 us)
Async XLA Ops:
  0.6 106.8 %collective-permute-start.2 = (f32[1]{0:T(128)}, f32[1]{0:T(128)}, u32[]{:S(2)}, u32[]{:S(2)}) collective-permute-start(f32[1]{0:T(128)} %param.9), channel_id=1, source_target_pairs={{0,0},{2,2},{4,32},{6,34},{8,64},{10,66},{12,96},{14,98},{16,128},... | collective-permute-start | bytes 20 | tf_op jit(solution)/shard_map/ppermute | solution.py:767
  10.6 95.9 %collective-permute-start = (s32[256]{0:T(256)S(1)}, s32[256]{0:T(256)S(1)}, u32[]{:S(2)}, u32[]{:S(2)}) collective-permute-start(s32[256]{0:T(256)S(1)} %reshape_squeeze.3.kept), channel_id=1, source_target_pairs={{0,0},{2,2},{4,32},{6,34},{8,64},{10,66},{12,96},{14,98},{16,128},... | collective-permute-start | bytes 3080 | tf_op jit(solution)/shard_map/ppermute | solution.py:766
  108.3 3.3 %collective-permute-start.1 = (s32[256]{0:T(256)S(1)}, s32[256]{0:T(256)S(1)}, u32[]{:S(2)}, u32[]{:S(2)}) collective-permute-start(s32[256]{0:T(256)S(1)} %collective-permute-done), channel_id=1, source_target_pairs={{0,2},{2,0},{4,6},{6,4},{8,10},{10,8},{12,14},{14,12},{16,18},{18,... | collective-permute-start | bytes 3080 | tf_op jit(solution)/shard_map/ppermute | solution.py:769

commit v4 on v3

--- a/solution.py
+++ b/solution.py
@@ -150,7 +150,7 @@
     )
     ring.start(first, None)
     y = yh * 2 + p
-    batches = [4, 2, 3, 2, 2, 2]
+    batches = [4, 2, 2, 2, 2, 2, 1]
 
     def plane(dx, dy):
         ty = (y + dy) % 4
@@ -193,6 +193,7 @@
     sent.append(push(firstz.at[p, af], firstz.at[p, af], b_send.at[7], b_recv.at[7], across))
     send_some()
     ring.step(1)
+    send_some()
     relay(1, al)
     relay(2, ar)
     ring.step(2)
@@ -240,10 +241,6 @@
     )(second, first)
 
 
-def tile_of(ref, lead, block):
-    return ref[(*lead, slice(None), pl.ds(pl.multiple_of(block // 2 * LANES, LANES), LANES))]
-
-
 def load_tiles(sec_hbm, sec, sem):
     return [
         pltpu.make_async_copy(sec_hbm.at[:, :, pl.ds(t * LANES, LANES)], sec.at[:, t], sem.at[t])
@@ -260,14 +257,13 @@
 
 
 def amplitude_kernel(
-    naux, nz, nb, tiles, sec_hbm, first_hbm, straight, divisor, amp1, amp2,
+    naux, nz, nb, tiles, sec_hbm, first_hbm, straight, divisor, amp, mine,
     sec, first, own, other, twin, outgoing, got, shard,
-    d_send, d_recv, r_send, r_recv, t_send, t_recv, x_send, x_recv, s_load, loc, *sems
+    d_send, d_recv, r_send, r_recv, t_send, t_recv, s_load, loc, *sems
 ):
     a, z, c, p = place()
-    x, yh = a // 2, a % 2
     size = divisor.shape[0]
-    loads = [pltpu.make_async_copy(first_hbm, first, loc.at[2]), *load_tiles(sec_hbm, sec, s_load)]
+    loads = [pltpu.make_async_copy(first_hbm, first, loc.at[0]), *load_tiles(sec_hbm, sec, s_load)]
     for load in loads:
         load.start()
     far, half = nz // 2, size // 2
@@ -276,24 +272,8 @@
         return device(a, (z + dz) % nz, (c + dc) % 2, p)
 
     sibling = me(0, 1)
-    mirror = device(z, a, c, p)
-    barrier = pltpu.get_barrier_semaphore()
-    line = [
-        device((x + dx) % NX * 2 + (yh + dy) % 2, z, c, p) for dx, dy in LINE
-    ]
-    peers = [sibling, me(1, 0), me(nz - 1, 0)] + line
-    for peer in peers:
-        pl.semaphore_signal(barrier, inc=1, device_id=peer, device_id_type=MESH)
-
-    @pl.when(a != z)
-    def _():
-        pl.semaphore_signal(barrier, inc=1, device_id=mirror, device_id_type=MESH)
-        pl.semaphore_wait(barrier, len(peers) + 1)
-
-    @pl.when(a == z)
-    def _():
-        pl.semaphore_wait(barrier, len(peers))
-
+    line = [device((a + da) % naux, z, c, p) for da in range(1, naux)]
+    greet([sibling, me(1, 0), me(nz - 1, 0)] + line)
     for load in loads:
         load.wait()
     lane = lax.broadcasted_iota(jnp.int32, (BLK, LANES), 1)
@@ -394,43 +374,51 @@
     lax.fori_loop(0, size, reduce, 0, unroll=2)
 
     ring = Ring(
-        lambda zz, cc: amp1.at[cc, pl.ds(zz * size, size)],
-        lambda zz, cc, h: amp1.at[cc, pl.ds(zz * size + h * half, half)],
+        lambda zz, cc: amp.at[cc, pl.ds(zz * size, size)],
+        lambda zz, cc, h: amp.at[cc, pl.ds(zz * size + h * half, half)],
         z, nz, c, lambda dz, dc: me((dz + nz) % nz, dc), sems,
     )
+    ring.start(shard, None)
+    here = pltpu.make_async_copy(shard, amp.at[c, rows(z)], loc.at[1])
+    here.start()
+
+    keep = pltpu.make_async_copy(shard, mine, loc.at[2])
+
+    @pl.when(a == z)
+    def _():
+        keep.start()
+
+    def hand_out(n, start):
+        s = (z + n) % nz
+        copy = pltpu.make_async_remote_copy(
+            src_ref=amp.at[c, rows(s)], dst_ref=mine, send_sem=t_send.at[n - 1],
+            recv_sem=t_recv.at[0], device_id=device(s, z, c, p), device_id_type=MESH,
+        )
+        if start:
+            copy.start()
+        else:
+            copy.wait_send()
+
+    for step in range(far):
+        ring.step(step)
+
+        @pl.when(a == z)
+        def _():
+            for n in sorted({step + 1, nz - 1 - step}):
+                hand_out(n, True)
+
+    ring.finish()
+
+    @pl.when(a == z)
+    def _():
+        keep.wait()
+        for n in range(1, nz):
+            hand_out(n, False)
+
     @pl.when(a != z)
     def _():
-        push(shard, amp2.at[z], t_send.at[0], t_recv.at[0], mirror)
-
-    @pl.when(a == z)
-    def _():
-        pltpu.make_async_copy(shard, amp2.at[z], loc.at[0]).start()
-
-    ring.start(shard, None)
-    here = pltpu.make_async_copy(shard, amp1.at[c, rows(z)], loc.at[1])
-    here.start()
-    ring.step(0)
-
-    @pl.when(a != z)
-    def _():
-        landed(amp2.at[a], t_send.at[0], t_recv.at[0], mirror)
-        pltpu.make_async_remote_copy(
-            src_ref=shard, dst_ref=amp2.at[z], send_sem=t_send.at[0], recv_sem=t_recv.at[0],
-            device_id=mirror, device_id_type=MESH,
-        ).wait_send()
-
-    @pl.when(a == z)
-    def _():
-        pltpu.make_async_copy(shard, amp2.at[z], loc.at[0]).wait()
-
-    for n, peer in enumerate(line):
-        sent.append(push(amp2.at[a], amp2.at[a], x_send.at[n], x_recv.at[n], peer))
-    for step in range(1, far):
-        ring.step(step)
-    ring.finish()
-    for n, (dx, dy) in enumerate(LINE):
-        fa = (x - dx + NX) % NX * 2 + (yh + dy) % 2
-        landed(amp2.at[fa], x_send.at[n], x_recv.at[n], device(fa, z, c, p))
+        landed(mine, t_send.at[0], t_recv.at[0], device(z, z, c, p))
+
     here.wait()
     for copy in sent:
         copy.wait_send()
@@ -449,7 +437,7 @@
         functools.partial(amplitude_kernel, naux, nz, nb),
         out_shape=[
             jax.ShapeDtypeStruct((2, entries, *block), BF16),
-            jax.ShapeDtypeStruct((naux, size, *block), BF16),
+            jax.ShapeDtypeStruct((size, *block), BF16),
         ],
         in_specs=[pl.BlockSpec(memory_space=pltpu.SMEM), hbm, hbm, vmem, vmem],
         out_specs=[hbm, hbm],
@@ -462,8 +450,8 @@
             pltpu.VMEM((2, nz // 2, size, *block), BF16),
             pltpu.VMEM((2, nz // 2, size, *block), BF16),
             pltpu.VMEM((size, *block), BF16),
-            dma((nz,)), dma((nz,)), dma((2, nz // 2, 2)), dma((2, nz // 2, 2)), dma((1,)), dma((1,)),
-            dma((naux - 1,)), dma((naux - 1,)), dma((width // LANES,)), dma((3,)),
+            dma((nz,)), dma((nz,)), dma((2, nz // 2, 2)), dma((2, nz // 2, 2)),
+            dma((nz - 1,)), dma((1,)), dma((width // LANES,)), dma((3,)),
             *ring_sems(nz),
         ],
         compiler_params=pltpu.CompilerParams(
@@ -473,15 +461,6 @@
     )(tiles, sec, first, straight, divisor)
 
 
-def spread_halves(amp, b0, b1):
-    lane = lax.broadcasted_iota(jnp.int32, (BLK, LANES), 1) // BLK
-    turned = pltpu.roll(amp, BLK, 1)
-    zero = jnp.zeros_like(amp)
-    t0 = jnp.where(lane == b0 % 2, jnp.where(b0 % 2 == 0, amp, turned), zero)
-    t1 = jnp.where(lane == b1 % 2, jnp.where(b1 % 2 == 1, amp, turned), zero)
-    return t0, t1
-
-
 class Sum:
     def __init__(self, me, up, dn, s0, r0, s1, r1):
         self.me, self.up, self.dn = me, up, dn
@@ -510,9 +489,9 @@
 
 
 def first_density_kernel(
-    naux, nz, nb, tiles, sec_hbm, amp_hbm, straight, out,
+    naux, nz, nb, tiles, sec_hbm, amp_hbm, mine, straight, out, amps,
     sec, amp, part, got_a, give_b, got_b, total, give_c, got_c, give_d, got_d, done,
-    p1s, p1r, p2s, p2r, z_send, z_recv, s_load, loc
+    p1s, p1r, p2s, p2r, z_send, z_recv, x_send, x_recv, s_load, loc
 ):
     a, z, c, p = place()
     loads = [pltpu.make_async_copy(amp_hbm, amp, loc.at[0]), *load_tiles(sec_hbm, sec, s_load)]
@@ -532,10 +511,17 @@
     column = [(dz, dc) for dz in range(nz) for dc in range(2) if (dz, dc) != (0, 0)]
     right, left = device((a + 2) % naux, z, c, p), device((a + naux - 2) % naux, z, c, p)
     above, below = at_y((y + 1) % 4), at_y((y + 3) % 4)
-    greet([right, left, above, below] + [me(dz, dc) for dz, dc in column])
+    yh = a % 2
+    line = [device((x + dx) % NX * 2 + (yh + dy) % 2, z, c, p) for dx, dy in LINE]
+    greet(line + [above, below] + [me(dz, dc) for dz, dc in column])
+    keep = pltpu.make_async_copy(mine, amps.at[a], loc.at[2])
+    keep.start()
     for load in loads:
         load.wait()
     sent = []
+
+    def pass_on(n):
+        sent.append(push(mine, amps.at[a], x_send.at[n], x_recv.at[n], line[n]))
 
     def compute(k):
         chunk = (z + 1 + k) % nz
@@ -645,13 +631,16 @@
                     push(source, out.at[z * 2 + c], z_send.at[n], z_recv.at[n], me(dz, dc))
                 )
 
-    stages = (stage_b, stage_c, stage_d, stage_e, stage_f)
-    for k in range(nz + len(stages) - 1):
+    stages = ((stage_b, 0), (stage_c, 2), (stage_d, 5), (stage_e, 7), (stage_f, 9))
+    waiting = list(range(len(line)))
+    for k in range(nz + stages[-1][1]):
         if k < nz:
             compute(k)
-        for lag, stage in enumerate(stages):
+        for stage, lag in stages:
             if 0 <= k - lag < nz:
                 stage(k - lag)
+        if waiting:
+            pass_on(waiting.pop(0))
 
     for dz, dc in column:
         fz, fc = (z - dz + nz) % nz, (c + dc) % 2
@@ -661,11 +650,15 @@
         done.at[nz - 1, :, pl.ds(pl.multiple_of(c * chunk_half, chunk_half), chunk_half)],
         out.at[z * 2 + c], loc.at[1],
     ).wait()
+    keep.wait()
+    for n, (dx, dy) in enumerate(LINE):
+        fa = (x - dx + NX) % NX * 2 + (yh + dy) % 2
+        landed(amps.at[fa], x_send.at[n], x_recv.at[n], device(fa, z, c, p))
     for copy in sent:
         copy.wait_send()
 
 
-def first_density_of(tiles, sec, amp, straight, naux, nz):
+def first_density_of(tiles, sec, amp, mine, straight, naux, nz):
     _, rows, width = sec.shape
     nb = width // BLK
     frows, chunk = rows // naux, width // nz
@@ -673,11 +666,15 @@
     hbm = pl.BlockSpec(memory_space=pl.ANY)
     return pl.pallas_call(
         functools.partial(first_density_kernel, naux, nz, nb),
-        out_shape=jax.ShapeDtypeStruct((nz * 2, frows, chunk // 2), BF16),
+        out_shape=[
+            jax.ShapeDtypeStruct((nz * 2, frows, chunk // 2), BF16),
+            jax.ShapeDtypeStruct((naux, *mine.shape), BF16),
+        ],
         in_specs=[
-            pl.BlockSpec(memory_space=pltpu.SMEM), hbm, hbm, pl.BlockSpec(memory_space=pltpu.VMEM)
+            pl.BlockSpec(memory_space=pltpu.SMEM), hbm, hbm, hbm,
+            pl.BlockSpec(memory_space=pltpu.VMEM),
         ],
-        out_specs=hbm,
+        out_specs=[hbm, hbm],
         scratch_shapes=[
             pltpu.VMEM((2, width // LANES, rows, LANES), BF16),
             pltpu.VMEM(amp.shape, BF16),
@@ -692,13 +689,14 @@
             pltpu.VMEM((nz, 2, frows, chunk), BF16),
             pltpu.VMEM((nz, frows, chunk), BF16),
             dma((nz, 2, 2)), dma((nz, 2, 2)), dma((nz, 2, 2)), dma((nz, 2, 2)),
-            dma((nz * 2,)), dma((nz * 2,)), dma((width // LANES,)), dma((2,)),
+            dma((nz * 2,)), dma((nz * 2,)), dma((naux - 1,)), dma((naux - 1,)),
+            dma((width // LANES,)), dma((3,)),
         ],
         compiler_params=pltpu.CompilerParams(
             collective_id=3, has_side_effects=True, vmem_limit_bytes=VMEM_LIMIT
         ),
         name="first_density",
-    )(tiles, sec, amp, straight)
+    )(tiles, sec, amp, mine, straight)
 
 
 def toward_second_kernel(group, nb, kept, first, amp, out, total):
@@ -708,24 +706,32 @@
     def _():
         total[...] = jnp.zeros_like(total)
 
-    nothing = jnp.zeros((BLK, 2 * LANES), BF16)
+    lane = lax.broadcasted_iota(jnp.int32, (LANES, LANES), 1)
     for pairs in range(group // 2):
         left = first[0, :, pairs * LANES:(pairs + 1) * LANES]
-        for e in range(2):
-            entry = pairs * 2 + e
-            at = (i * nb + g * group + entry) * 2
-            b0, b1 = kept[at], kept[at + 1]
-            t0, t1 = spread_halves(amp[entry].astype(F32), b0, b1)
-            weights = jnp.concatenate([t0, t1], axis=1).astype(BF16)
-            stack = [weights, nothing] if e == 0 else [nothing, weights]
-            term = jnp.dot(left, jnp.concatenate(stack, axis=0), preferred_element_type=F32)
-            for b, part in ((b0, term[:, :LANES]), (b1, term[:, LANES:])):
-                at_lanes = pl.ds(pl.multiple_of(b // 2 * LANES, LANES), LANES)
-                total[:, at_lanes] += part
+        turned = jnp.concatenate(
+            [amp[pairs * 2].astype(F32), amp[pairs * 2 + 1].astype(F32)], axis=0
+        ).T
+        zero = jnp.zeros_like(turned)
+        weights = jnp.concatenate(
+            [jnp.where(lane < BLK, turned, zero), jnp.where(lane < BLK, zero, turned)], axis=0
+        ).astype(BF16)
+        term = lax.dot_general(
+            weights, left, (((1,), (1,)), ((), ())), preferred_element_type=F32
+        )
+        for n in range(4):
+            b = kept[(i * nb + g * group + pairs * 2) * 2 + n]
+            at_rows = pl.ds(pl.multiple_of(b * BLK, BLK), BLK)
+            total[at_rows, :] += term[n * BLK:(n + 1) * BLK]
 
     @pl.when((i == pl.num_programs(0) - 1) & (g == pl.num_programs(1) - 1))
     def _():
-        out[...] = total[...].astype(BF16)
+        def turn(t, _):
+            cols = pl.ds(pl.multiple_of(t * LANES, LANES), LANES)
+            out[:, cols] = total[cols, :].T.astype(BF16)
+            return 0
+
+        lax.fori_loop(0, out.shape[1] // LANES, turn, 0, unroll=2)
 
 
 def toward_second(kept, first, amp, group=8):
@@ -743,7 +749,7 @@
                 pl.BlockSpec((group, BLK, LANES), lambda i, g, kept: (i * groups + g, 0, 0)),
             ],
             out_specs=pl.BlockSpec((rows, width), lambda i, g, kept: (0, 0)),
-            scratch_shapes=[pltpu.VMEM((rows, width), F32)],
+            scratch_shapes=[pltpu.VMEM((width, rows), F32)],
         ),
         compiler_params=pltpu.CompilerParams(vmem_limit_bytes=VMEM_LIMIT),
         name="toward_second",
@@ -788,8 +794,8 @@
     firstz = firstz.reshape(ni, naux * frows, width)
     firsta = firsta.reshape(ni, nz * 2 * frows, width)
 
-    amp1, amp2 = amplitudes(tiles, sec, firstz, straight, divisor, naux, nz)
-    first_density = first_density_of(tiles, sec, amp1, straight, naux, nz)
+    amp1, mine = amplitudes(tiles, sec, firstz, straight, divisor, naux, nz)
+    first_density, amp2 = first_density_of(tiles, sec, amp1, mine, straight, naux, nz)
     amp2 = amp2.reshape(entries, BLK, LANES)
     second_density = toward_second(kept_here, firsta, amp2)
     return (

time: 295 us -> 282 us (0.956)
  Pallas kernels: 258 us -> 244 us
    pallas_call x1, Pallas kernels: 94.6 us -> 70.1 us  [amplitudes(): pl.pallas_call(functools.partial(amplitude_kernel, naux, nz, nb), out_sha...]
    pallas_call x1, Pallas kernels: 54.3 us -> 75.2 us  [first_density_of(): pl.pallas_call(functools.partial(first_density_kernel, naux, nz, nb), out...]
    pallas_call x1, Pallas kernels: 29.8 us -> 18.8 us  [toward_second(): pl.pallas_call(functools.partial(toward_second_kernel, group, nb), out_sh...]
    ppermute x1, starting transfers between devices: 4.11 us -> 8.99 us  [shards(): kept_mine = lax.ppermute(kept_here, ('aux', 'occ'), order)]
    ppermute x1, starting transfers between devices: 8.99 us -> 4.11 us  [shards(): energy_mine = lax.ppermute(second_energy, ('aux', 'occ'), order)]
  transfers between devices with their start and end apart: 3 -> 3, of which waited for: 1 -> 1; matrix products, arithmetic and copies ran while one was open for 5% -> 4% of each run, Pallas kernels for 27% -> 29%
where the time goes in v4:
time: 282 us; the launch traced here: 276 us
  Pallas kernels  244 us (87%)
  starting transfers between devices  15.6 us (6%)
  local copies, waits for them, and re-layouts  12.6 us (4%)
    pallas_call x1, Pallas kernels, spread(): pl.pallas_call(functools.partial(spread_kernel, naux, nz), out_shape=[jax...  80.1 us
    pallas_call x1, Pallas kernels, first_density_of(): pl.pallas_call(functools.partial(first_density_kernel, naux, nz, nb), out...  75.2 us
    pallas_call x1, Pallas kernels, amplitudes(): pl.pallas_call(functools.partial(amplitude_kernel, naux, nz, nb), out_sha...  70.1 us
    pallas_call x1, Pallas kernels, toward_second(): pl.pallas_call(functools.partial(toward_second_kernel, group, nb), out_sh...  18.8 us
    ppermute x1, starting transfers between devices, shards(): kept_mine = lax.ppermute(kept_here, ('aux', 'occ'), order)  8.99 us
    transpose x1, local copies, waits for them, and re-layouts, shards(): jnp.transpose(second_factors, (1, 0, 2)).reshape(naux, 2, 2, rows, width)  6.56 us
  transfers between devices with their start and end apart: 3, of which 1 were waited for; matrix products, arithmetic and copies ran while one was open for 4% of the time, Pallas kernels for 29%

profile of v4, /device:TPU:29, one launch (start us, length us, event | category | flops | bytes accessed | tf_op | source)
XLA Modules:
  0.0 276.4 jit_solution(4128090233583380333)
XLA Ops:
  0.6 0.8 copy.10
  1.4 0.1 reshape_squeeze.3.kept
  1.6 9.0 %collective-permute-start = (s32[256]{0:T(256)S(1)}, s32[256]{0:T(256)S(1)}, u32[]{:S(2)}, u32[]{:S(2)}) collective-permute-start(s32[256]{0:T(256)S(1)} %reshape_squeeze.3.kept), channel_id=1, source_target_pairs={{0,0},{2,2},{4,32},{6,34},{8,64},{10,66},{12,96},{14,98},{16,128},... | collective-permute-start | bytes 3080 | tf_op jit(solution)/shard_map/ppermute | solution.py:772
  10.6 4.1 %collective-permute-start.2 = (f32[1]{0:T(128)}, f32[1]{0:T(128)}, u32[]{:S(2)}, u32[]{:S(2)}) collective-permute-start(f32[1]{0:T(128)} %param.9), channel_id=1, source_target_pairs={{0,0},{2,2},{4,32},{6,34},{8,64},{10,66},{12,96},{14,98},{16,128},... | collective-permute-start | bytes 20 | tf_op jit(solution)/shard_map/ppermute | solution.py:773
  14.7 1.3 fusion.8
  16.0 0.8 reshape.198
  16.8 0.6 gather_fusion
  17.5 1.3 and_select_fusion.1
  18.8 6.6 %copy.11 = bf16[32,16,4096]{2,1,0:T(8,128)(2,1)} copy(bf16[32,16,4096]{2,0,1:T(8,128)(2,1)} %bitcast.32) | data formatting | bytes 8388608 | tf_op jit(solution)/shard_map/transpose | solution.py:790
  25.4 0.3 copy.16
  25.7 80.1 %spread.1 = (bf16[2,16,16,4096]{3,2,1,0:T(8,128)(2,1)}, bf16[2,8,32,4096]{3,2,1,0:T(8,128)(2,1)}, bf16[2,16,32,4096]{3,2,1,0:T(8,128)(2,1)}) custom-call(bf16[8,2,2,16,4096]{4,3,2,1,0:T(8,128)(2,1)} %bitcast.29, bf16[2,32,4096]{2,1,0:T(8,128)(2,1)S(1)} %bitcast.25), custom_call_target="tpu_custom_call" | custom-call | tf_op jit(solution)/shard_map/spread/pallas_call | solution.py:220
  105.9 0.1 broadcast_in_dim.36
  106.0 0.1 broadcast_in_dim.37
  106.2 0.6 gather_fusion.1
  106.8 0.8 subtract_subtract_fusion.divisor
  107.6 2.5 collective-permute-start.1
  110.1 0.8 collective-permute-done.1
  110.9 0.2 slice.7
  111.1 0.2 slice.6
  111.5 0.1 copy.13.straight
  111.6 70.1 %amplitudes.1 = (bf16[2,128,64,128]{3,2,1,0:T(8,128)(2,1)}, bf16[16,64,128]{2,1,0:T(8,128)(2,1)S(1)}) custom-call(s32[512]{0:T(512)S(1)} %add_select_fusion.tiles, bf16[2,256,4096]{2,1,0:T(8,128)(2,1)} %bitcast.27, bf16[2,256,4096]{2,1,0:T(8,128)(2,1)} %bitcast.31, f32[256,128]{1,0:T(8,128)S(1)} %copy.13.straight, ...), custom_call_target="tpu_custom_call" | custom-call | tf_op jit(solution)/shard_map/amplitudes/pallas_call | solution.py:436
  181.7 75.2 %first_density.1 = (bf16[16,32,256]{2,1,0:T(8,128)(2,1)S(1)}, bf16[8,16,64,128]{3,2,1,0:T(8,128)(2,1)}) custom-call(s32[512]{0:T(512)S(1)} %add_select_fusion.tiles, bf16[2,256,4096]{2,1,0:T(8,128)(2,1)} %bitcast.28, bf16[2,128,64,128]{3,2,1,0:T(8,128)(2,1)} %get-tuple-element.11.amp_hbm, bf16[16,64,128]{2,1,0:T(8,128)(2,1)S(1)} %get-tuple-element.12.mine, ...), custom_call_target="tpu_custom_call" | custom-call | tf_op jit(solution)/shard_map/first_density/pallas_call | solution.py:667
  256.9 18.8 %toward_second.1 = bf16[512,4096]{1,0:T(8,128)(2,1)} custom-call(s32[256]{0:T(256)S(1)} %reshape_squeeze.3.kept, bf16[2,512,4096]{2,1,0:T(8,128)(2,1)} %bitcast.30, bf16[128,64,128]{2,1,0:T(8,128)(2,1)} %bitcast.34), custom_call_target="tpu_custom_call" | custom-call | tf_op jit(solution)/shard_map/toward_second/pallas_call | solution.py:741
  275.7 0.7 copy.20
  (23 shorter events, 0.5 us)
Async XLA Ops:
  1.6 104.2 %collective-permute-start = (s32[256]{0:T(256)S(1)}, s32[256]{0:T(256)S(1)}, u32[]{:S(2)}, u32[]{:S(2)}) collective-permute-start(s32[256]{0:T(256)S(1)} %reshape_squeeze.3.kept), channel_id=1, source_target_pairs={{0,0},{2,2},{4,32},{6,34},{8,64},{10,66},{12,96},{14,98},{16,128},... | collective-permute-start | bytes 3080 | tf_op jit(solution)/shard_map/ppermute | solution.py:772
  10.6 96.3 %collective-permute-start.2 = (f32[1]{0:T(128)}, f32[1]{0:T(128)}, u32[]{:S(2)}, u32[]{:S(2)}) collective-permute-start(f32[1]{0:T(128)} %param.9), channel_id=1, source_target_pairs={{0,0},{2,2},{4,32},{6,34},{8,64},{10,66},{12,96},{14,98},{16,128},... | collective-permute-start | bytes 20 | tf_op jit(solution)/shard_map/ppermute | solution.py:773
  18.8 6.6 %copy-start = (bf16[32,2,4096]{2,1,0:T(2,128)(2,1)S(1)}, bf16[32,2,4096]{2,1,0:T(2,128)(2,1)}, u32[]{:S(2)}) copy-start(bf16[32,2,4096]{2,1,0:T(2,128)(2,1)} %param.6) | copy-start | bytes 1572868
  107.6 3.3 %collective-permute-start.1 = (s32[256]{0:T(256)S(1)}, s32[256]{0:T(256)S(1)}, u32[]{:S(2)}, u32[]{:S(2)}) collective-permute-start(s32[256]{0:T(256)S(1)} %collective-permute-done), channel_id=1, source_target_pairs={{0,2},{2,0},{4,6},{6,4},{8,10},{10,8},{12,14},{14,12},{16,18},{18,... | collective-permute-start | bytes 3080 | tf_op jit(solution)/shard_map/ppermute | solution.py:775

commit v5 on v4

--- a/solution.py
+++ b/solution.py
@@ -734,7 +734,7 @@
         lax.fori_loop(0, out.shape[1] // LANES, turn, 0, unroll=2)
 
 
-def toward_second(kept, first, amp, group=8):
+def toward_second(kept, first, amp, group=16):
     ni, rows, width = first.shape
     nb = width // BLK
     groups = nb // group
@@ -771,8 +771,8 @@
     kept_here = kept_blocks[:, 0].reshape(entries * 2)
     kept_mine = lax.ppermute(kept_here, ("aux", "occ"), order)
     energy_mine = lax.ppermute(second_energy, ("aux", "occ"), order)
-    swap = [(o, o // 2 * 2 + 1 - o % 2) for o in range(2 * nz)]
-    kept_twin = lax.ppermute(kept_mine, "occ", swap)
+    crossed = [(source, target + 1 - 2 * (target % 2)) for source, target in order]
+    kept_twin = lax.ppermute(kept_here, ("aux", "occ"), crossed)
     kept = jnp.concatenate([kept_mine, kept_twin])
     tiles = kept // 2
     in_place = jnp.stack([kept[0::2] % 2 == 0, kept[1::2] % 2 == 1], axis=1)

time: 282 us -> 285 us (1.011)
  starting transfers between devices: 15.6 us -> 21.1 us
    ppermute x1, starting transfers between devices: 4.11 us -> 8.98 us  [shards(): energy_mine = lax.ppermute(second_energy, ('aux', 'occ'), order)]
    pallas_call x1, Pallas kernels: 18.8 us -> 14.8 us  [toward_second(): pl.pallas_call(functools.partial(toward_second_kernel, group, nb), out_sh...]
  transfers between devices with their start and end apart: 3 -> 3, of which waited for: 1 -> 0; matrix products, arithmetic and copies ran while one was open for 4% -> 4% of each run, Pallas kernels for 29% -> 29%
where the time goes in v5:
time: 285 us; the launch traced here: 281 us
  Pallas kernels  244 us (86%)
  starting transfers between devices  21.1 us (7%)
  local copies, waits for them, and re-layouts  12.6 us (4%)
    pallas_call x1, Pallas kernels, spread(): pl.pallas_call(functools.partial(spread_kernel, naux, nz), out_shape=[jax...  80.8 us
    pallas_call x1, Pallas kernels, first_density_of(): pl.pallas_call(functools.partial(first_density_kernel, naux, nz, nb), out...  77.6 us
    pallas_call x1, Pallas kernels, amplitudes(): pl.pallas_call(functools.partial(amplitude_kernel, naux, nz, nb), out_sha...  70.6 us
    pallas_call x1, Pallas kernels, toward_second(): pl.pallas_call(functools.partial(toward_second_kernel, group, nb), out_sh...  14.8 us
    ppermute x1, starting transfers between devices, shards(): kept_mine = lax.ppermute(kept_here, ('aux', 'occ'), order)  8.99 us
    ppermute x1, starting transfers between devices, shards(): energy_mine = lax.ppermute(second_energy, ('aux', 'occ'), order)  8.98 us
    transpose x1, local copies, waits for them, and re-layouts, shards(): jnp.transpose(second_factors, (1, 0, 2)).reshape(naux, 2, 2, rows, width)  6.56 us
  transfers between devices with their start and end apart: 3, of which 0 were waited for; matrix products, arithmetic and copies ran while one was open for 4% of the time, Pallas kernels for 29%

profile of v5, /device:TPU:29, one launch (start us, length us, event | category | flops | bytes accessed | tf_op | source)
XLA Modules:
  0.0 280.7 jit_solution(3083007586236660843)
XLA Ops:
  0.6 0.8 copy.10
  1.4 0.1 reshape_squeeze.3.kept
  1.6 9.0 %collective-permute-start = (s32[256]{0:T(256)S(1)}, s32[256]{0:T(256)S(1)}, u32[]{:S(2)}, u32[]{:S(2)}) collective-permute-start(s32[256]{0:T(256)S(1)} %reshape_squeeze.3.kept), channel_id=1, source_target_pairs={{0,0},{2,2},{4,32},{6,34},{8,64},{10,66},{12,96},{14,98},{16,128},... | collective-permute-start | bytes 3080 | tf_op jit(solution)/shard_map/ppermute | solution.py:772
  10.6 3.1 %collective-permute-start.1 = (s32[256]{0:T(256)S(1)}, s32[256]{0:T(256)S(1)}, u32[]{:S(2)}, u32[]{:S(2)}) collective-permute-start(s32[256]{0:T(256)S(1)} %reshape_squeeze.3.kept), channel_id=1, source_target_pairs={{0,2},{2,0},{4,34},{6,32},{8,66},{10,64},{12,98},{14,96},{16,130},... | collective-permute-start | bytes 3080 | tf_op jit(solution)/shard_map/ppermute | solution.py:775
  13.7 9.0 %collective-permute-start.2 = (f32[1]{0:T(128)}, f32[1]{0:T(128)}, u32[]{:S(2)}, u32[]{:S(2)}) collective-permute-start(f32[1]{0:T(128)} %param.9), channel_id=1, source_target_pairs={{0,0},{2,2},{4,32},{6,34},{8,64},{10,66},{12,96},{14,98},{16,128},... | collective-permute-start | bytes 20 | tf_op jit(solution)/shard_map/ppermute | solution.py:773
  22.7 1.3 fusion.8
  24.0 0.8 reshape.198
  24.8 0.6 gather_fusion
  25.5 1.3 and_select_fusion.1
  26.8 6.6 %copy.11 = bf16[32,16,4096]{2,1,0:T(8,128)(2,1)} copy(bf16[32,16,4096]{2,0,1:T(8,128)(2,1)} %bitcast.32) | data formatting | bytes 8388608 | tf_op jit(solution)/shard_map/transpose | solution.py:790
  33.4 0.3 copy.16
  33.7 80.8 %spread.1 = (bf16[2,16,16,4096]{3,2,1,0:T(8,128)(2,1)}, bf16[2,8,32,4096]{3,2,1,0:T(8,128)(2,1)}, bf16[2,16,32,4096]{3,2,1,0:T(8,128)(2,1)}) custom-call(bf16[8,2,2,16,4096]{4,3,2,1,0:T(8,128)(2,1)} %bitcast.29, bf16[2,32,4096]{2,1,0:T(8,128)(2,1)S(1)} %bitcast.25), custom_call_target="tpu_custom_call" | custom-call | tf_op jit(solution)/shard_map/spread/pallas_call | solution.py:220
  114.5 0.2 slice.7
  114.7 0.2 slice.6
  115.0 0.1 copy.13.straight
  115.2 0.1 broadcast_in_dim.36
  115.3 0.1 broadcast_in_dim.37
  115.4 0.1 broadcast_in_dim.38
  115.5 0.6 gather_fusion.1
  116.2 0.8 subtract_subtract_fusion.divisor
  116.9 70.6 %amplitudes.1 = (bf16[2,128,64,128]{3,2,1,0:T(8,128)(2,1)}, bf16[16,64,128]{2,1,0:T(8,128)(2,1)S(1)}) custom-call(s32[512]{0:T(512)S(1)} %add_select_fusion.tiles, bf16[2,256,4096]{2,1,0:T(8,128)(2,1)} %bitcast.27, bf16[2,256,4096]{2,1,0:T(8,128)(2,1)} %bitcast.31, f32[256,128]{1,0:T(8,128)S(1)} %copy.13.straight, ...), custom_call_target="tpu_custom_call" | custom-call | tf_op jit(solution)/shard_map/amplitudes/pallas_call | solution.py:436
  187.6 77.6 %first_density.1 = (bf16[16,32,256]{2,1,0:T(8,128)(2,1)S(1)}, bf16[8,16,64,128]{3,2,1,0:T(8,128)(2,1)}) custom-call(s32[512]{0:T(512)S(1)} %add_select_fusion.tiles, bf16[2,256,4096]{2,1,0:T(8,128)(2,1)} %bitcast.28, bf16[2,128,64,128]{3,2,1,0:T(8,128)(2,1)} %get-tuple-element.11.amp_hbm, bf16[16,64,128]{2,1,0:T(8,128)(2,1)S(1)} %get-tuple-element.12.mine, ...), custom_call_target="tpu_custom_call" | custom-call | tf_op jit(solution)/shard_map/first_density/pallas_call | solution.py:667
  265.2 14.8 %toward_second.1 = bf16[512,4096]{1,0:T(8,128)(2,1)} custom-call(s32[256]{0:T(256)S(1)} %reshape_squeeze.3.kept, bf16[2,512,4096]{2,1,0:T(8,128)(2,1)} %bitcast.30, bf16[128,64,128]{2,1,0:T(8,128)(2,1)} %bitcast.34), custom_call_target="tpu_custom_call" | custom-call | tf_op jit(solution)/shard_map/toward_second/pallas_call | solution.py:741
  280.0 0.7 copy.20
  (23 shorter events, 0.4 us)
Async XLA Ops:
  1.6 112.9 %collective-permute-start = (s32[256]{0:T(256)S(1)}, s32[256]{0:T(256)S(1)}, u32[]{:S(2)}, u32[]{:S(2)}) collective-permute-start(s32[256]{0:T(256)S(1)} %reshape_squeeze.3.kept), channel_id=1, source_target_pairs={{0,0},{2,2},{4,32},{6,34},{8,64},{10,66},{12,96},{14,98},{16,128},... | collective-permute-start | bytes 3080 | tf_op jit(solution)/shard_map/ppermute | solution.py:772
  10.6 103.9 %collective-permute-start.1 = (s32[256]{0:T(256)S(1)}, s32[256]{0:T(256)S(1)}, u32[]{:S(2)}, u32[]{:S(2)}) collective-permute-start(s32[256]{0:T(256)S(1)} %reshape_squeeze.3.kept), channel_id=1, source_target_pairs={{0,2},{2,0},{4,34},{6,32},{8,66},{10,64},{12,98},{14,96},{16,130},... | collective-permute-start | bytes 3080 | tf_op jit(solution)/shard_map/ppermute | solution.py:775
  13.7 102.5 %collective-permute-start.2 = (f32[1]{0:T(128)}, f32[1]{0:T(128)}, u32[]{:S(2)}, u32[]{:S(2)}) collective-permute-start(f32[1]{0:T(128)} %param.9), channel_id=1, source_target_pairs={{0,0},{2,2},{4,32},{6,34},{8,64},{10,66},{12,96},{14,98},{16,128},... | collective-permute-start | bytes 20 | tf_op jit(solution)/shard_map/ppermute | solution.py:773
  26.8 6.6 %copy-start = (bf16[32,2,4096]{2,1,0:T(2,128)(2,1)S(1)}, bf16[32,2,4096]{2,1,0:T(2,128)(2,1)}, u32[]{:S(2)}) copy-start(bf16[32,2,4096]{2,1,0:T(2,128)(2,1)} %param.6) | copy-start | bytes 1572868
